TPU v7x, 128 devices: a whole 4x4x4 slice. The times are simulated.
128 devices in a mesh: dp: 32 (over y, z, core), mp: 4 (over x).
Axes of the slice: x: 4, y: 4, z: 4, core: 2. Of those that a mesh axis runs over, the one named last changes fastest.
Arguments:
- features_table: bfloat16 [262144, 1024], P(('dp', 'mp')), may hold values from -6 to 6
- self_features: bfloat16 [4096, 1024], P(('dp', 'mp')), may hold values from -6 to 6
- neighbour_ids: int32 [4096, 32], P(('dp', 'mp')), may hold values from 0 to 262143, as said below
- neighbour_counts: int32 [4096], P(('dp', 'mp')), may hold values from 1 to 32
- node_owner: int32 [262144], replicated, may hold values from 0 to 127, as said below
- node_row: int32 [262144], replicated, may hold values from 0 to 2047, as said below
- list_ids: int32 [4096], P(('dp', 'mp')), may hold values from 0 to 1048575, as said below
- list_owner: int32 [1048576], replicated, may hold values from 0 to 127, as said below
- list_row: int32 [1048576], replicated, may hold values from 0 to 8191, as said below
- centroids: bfloat16 [1048576, 256], P(('dp', 'mp')), may hold values from -3 to 3
- w_self: bfloat16 [1024, 2048], P(None, 'mp'), may hold values from -0.1875 to 0.1875
- w_neigh: bfloat16 [1024, 2048], P(None, 'mp'), may hold values from -0.1875 to 0.1875
- w_query: bfloat16 [2048, 1024], P('mp'), may hold values from -0.5 to 0.5
- w_out: bfloat16 [2048, 256], P('mp'), may hold values from -0.125 to 0.125
- w_context: bfloat16 [1024, 256], replicated, may hold values from -0.375 to 0.375
Outputs:
- embedding: bfloat16 [4096, 256], P(('dp', 'mp'))
- residual_codes: float32 [16384, 2, 256], P(('dp', 'mp'))
Inputs may be any that keep to these rules, and one draw needn't show every extreme that they name: `neighbour_ids`: the neighbour slots of one device (its 32 new nodes, padded slots included) name nodes stored on any one device at most 16 times, and exactly 16 times for one storing device common to all devices. `node_owner`: each device stores exactly 2048 node ids. node_row numbers the ids of each device 0 to 2047, each once. `list_ids`: the 32 new nodes of one device are assigned to lists of any one owner at most 2 times, and exactly 2 times for one owner common to all devices. `list_owner`: each device owns exactly 8192 lists. list_row numbers the lists of each device 0 to 8191, each once.
All inputs are finite; a program needn't handle non-finite values.
Results may differ from a plain program's by a relative error of at most 0.0062.
Values may be sent and summed in bfloat16 or wider, within the bound.
A program may use at most 128 MiB of HBM per device.

v0:
```python
import math

import jax
import jax.numpy as jnp
from jax import lax
from jax.sharding import PartitionSpec as P


def rms_rows(values):
    return values * lax.rsqrt(jnp.mean(values * values, axis=-1, keepdims=True) + 1e-06)


def owner_ranks(owners, sources):
    total = owners.shape[0]
    ordering = jnp.argsort(owners, stable=True)
    sorted_owner = owners[ordering]
    per_owner = jnp.sum(
        (owners[:, None] == jnp.arange(sources, dtype=jnp.int32)[None, :]).astype(jnp.int32), axis=0
    )
    offsets = jnp.cumsum(per_owner) - per_owner
    rank_sorted = jnp.arange(total, dtype=jnp.int32) - offsets[sorted_owner]
    return jnp.zeros((total,), jnp.int32).at[ordering].set(rank_sorted)


def local(
    features_table,
    self_features,
    neighbour_ids,
    neighbour_counts,
    node_owner,
    node_row,
    list_ids,
    list_owner,
    list_row,
    centroids,
    w_self,
    w_neigh,
    w_query,
    w_out,
    w_context,
):
    sources = lax.axis_size(("dp", "mp"))
    new_loc, fanout = neighbour_ids.shape
    feature_w = features_table.shape[1]
    out_width = centroids.shape[1]
    cap_fetch = 2 * fanout * new_loc // sources
    cap_list = max(2, 2 * new_loc // sources)
    flat_ids = neighbour_ids.reshape(-1)
    fetch_owner = node_owner[flat_ids]
    fetch_row = node_row[flat_ids]
    fetch_rank = owner_ranks(fetch_owner, sources)
    list_dest = list_owner[list_ids]
    list_centre = list_row[list_ids]
    same_owner = list_dest[:, None] == list_dest[None, :]
    earlier = lax.broadcasted_iota(jnp.int32, (new_loc, new_loc), 1) < lax.broadcasted_iota(
        jnp.int32, (new_loc, new_loc), 0
    )
    list_rank = jnp.sum(jnp.logical_and(same_owner, earlier).astype(jnp.int32), axis=1)
    fetch_part = (
        jnp.zeros((sources, cap_fetch), jnp.int32).at[fetch_owner, fetch_rank].set(fetch_row)
    )
    list_part = (
        jnp.full((sources, cap_list), -1, jnp.int32).at[list_dest, list_rank].set(list_centre)
    )
    requests = jnp.concatenate([fetch_part, list_part], axis=1)
    incoming = lax.all_to_all(requests, ("dp", "mp"), split_axis=0, concat_axis=0, tiled=True)
    lookups = features_table[incoming[:, :cap_fetch]]
    returned = lax.all_to_all(
        lookups, ("dp", "mp"), split_axis=0, concat_axis=0, tiled=True
    ).reshape(sources * cap_fetch, feature_w)
    valid = (
        lax.broadcasted_iota(jnp.int32, (new_loc, fanout), 1) < neighbour_counts[:, None]
    ).reshape(-1)
    slot_node = lax.broadcasted_iota(jnp.int32, (new_loc, fanout), 0).reshape(-1)
    arrival = fetch_owner * cap_fetch + fetch_rank
    placement = (
        jnp.zeros((new_loc, sources * cap_fetch), jnp.float32)
        .at[slot_node, arrival]
        .add(valid.astype(jnp.float32))
    )
    counts_f = neighbour_counts.astype(jnp.float32)[:, None]
    masked_sums = jnp.dot(
        placement.astype(jnp.bfloat16), returned, preferred_element_type=jnp.float32
    )
    aggregate = (masked_sums / counts_f).astype(jnp.bfloat16)
    self_all, agg_all = (
        lax.all_gather(self_features, "mp", axis=0, tiled=True),
        lax.all_gather(aggregate, "mp", axis=0, tiled=True),
    )
    norm_self = rms_rows(self_all.astype(jnp.float32)).astype(jnp.bfloat16)
    norm_agg = rms_rows(agg_all.astype(jnp.float32)).astype(jnp.bfloat16)
    hidden = jax.nn.relu(
        jnp.dot(norm_self, w_self, preferred_element_type=jnp.float32)
        + jnp.dot(norm_agg, w_neigh, preferred_element_type=jnp.float32)
    ).astype(jnp.bfloat16)
    w_both = jnp.concatenate([w_query, w_out], axis=1)
    own_terms = lax.psum_scatter(
        jnp.dot(hidden, w_both, preferred_element_type=jnp.float32),
        "mp",
        scatter_dimension=0,
        tiled=True,
    )
    queries = own_terms[:, :feature_w].astype(jnp.bfloat16)
    head_part = own_terms[:, feature_w:]
    scores = lax.dot_general(
        queries, returned, (((1,), (1,)), ((), ())), preferred_element_type=jnp.float32
    ) / math.sqrt(feature_w)
    gates = jnp.where(placement > 0.5, jax.nn.sigmoid(scores), 0.0).astype(jnp.bfloat16)
    gated_sums = jnp.dot(gates, returned, preferred_element_type=jnp.float32)
    context = (gated_sums / counts_f).astype(jnp.bfloat16)
    pre_embed = head_part + jnp.dot(context, w_context, preferred_element_type=jnp.float32)
    embedding = rms_rows(pre_embed).astype(jnp.bfloat16)
    outbound = (
        jnp.zeros((sources, cap_list, out_width), jnp.bfloat16)
        .at[list_dest, list_rank]
        .set(embedding)
    )
    arrived = lax.all_to_all(outbound, ("dp", "mp"), split_axis=0, concat_axis=0, tiled=True)
    centre_index = incoming[:, cap_fetch:]
    centre_rows = centroids[jnp.maximum(centre_index, 0)]
    residual_codes = jnp.where(
        centre_index[:, :, None] >= 0,
        arrived.astype(jnp.float32) - centre_rows.astype(jnp.float32),
        0.0,
    )
    return (embedding, residual_codes)


def solution(mesh):
    placed = (
        P(("dp", "mp"), None),
        P(("dp", "mp"), None),
        P(("dp", "mp"), None),
        P(("dp", "mp")),
        P(),
        P(),
        P(("dp", "mp")),
        P(),
        P(),
        P(("dp", "mp"), None),
        P(None, "mp"),
        P(None, "mp"),
        P("mp", None),
        P("mp", None),
        P(),
    )
    return jax.shard_map(
        local,
        mesh=mesh,
        in_specs=placed,
        out_specs=(P(("dp", "mp"), None), P(("dp", "mp"), None, None)),
        check_vma=False,
    )
```

profile of v0, /device:TPU:1, one launch (start us, length us, event | category | flops | bytes accessed | tf_op | source)
XLA Modules:
  0.0 231.6 jit_solution(10843640769878629841)
XLA Ops:
  7.2 0.9 reshape.187
  8.1 13.4 %gather_fusion = s32[1024]{0:T(1024)S(1)} fusion(s32[262144]{0:T(1024)} %param.19, s32[1024]{0:T(1024)S(1)} %broadcast_clamp_fusion.3), kind=kCustom, calls=%fused_computation | custom fusion | bytes 12288 | tf_op jit(solution)/shard_map/gather | solution.py:49
  21.5 0.2 convert_reduce_fusion
  21.7 0.1 copy.25
  21.8 0.2 reduce-window.9
  22.0 0.1 reduce.4
  22.2 4.4 %sort.17 = (s32[1024]{0:T(1024)}, s32[1024]{0:T(1024)S(1)}) sort(s32[1024]{0:T(1024)S(1)} %gather_fusion, s32[1024]{0:T(1024)S(1)} %iota.32), dimensions={0}, to_apply=%region_1.2 | sort | flops 10240 | bytes 16384 | tf_op jit(solution)/shard_map/jit(argsort)/sort | solution.py:15
  26.5 4.5 %gather_fusion.1 = s32[1024]{0:T(1024)S(1)} fusion(s32[1024]{0:T(1024)S(1)} %gather_fusion, s32[1024]{0:T(1024)S(1)} %get-tuple-element.6), kind=kCustom, calls=%fused_computation.1 | custom fusion | bytes 12288 | tf_op jit(solution)/shard_map/gather | solution.py:16
  31.1 6.6 %gather_fusion.2 = s32[1024]{0:T(1024)S(1)} fusion(s32[128]{0:T(128)S(1)} %sub.9, s32[1024]{0:T(1024)S(1)} %broadcast_clamp_fusion.1), kind=kCustom, calls=%fused_computation.2 | custom fusion | bytes 12288 | tf_op jit(solution)/shard_map/gather | solution.py:21
  37.7 4.3 %scatter_custom_fusion = s32[1024]{0:T(1024)S(1)} fusion(s32[1024]{0:T(1024)S(1)} %get-tuple-element.7, s32[1024]{0:T(1024)S(1)} %iota_subtract_fusion, s32[]{:T(128)} %constant.21.clone.1), kind=kCustom, calls=%fused_computation.93 | custom fusion | bytes 4100 | tf_op jit(solution)/shard_map/scatter | solution.py:22
  42.1 0.1 multiply_reduce_fusion.1
  42.2 0.1 and_reduce_fusion
  42.3 6.2 %gather_fusion.3 = s32[1024]{0:T(1024)S(1)} fusion(s32[262144]{0:T(1024)S(1)} %copy-done.1, s32[1024]{0:T(1024)S(1)} %broadcast_clamp_fusion.3), kind=kCustom, calls=%fused_computation.3 | custom fusion | bytes 12288 | tf_op jit(solution)/shard_map/gather | solution.py:50
  48.5 1.6 gather_fusion.4
  50.0 0.2 convert_reduce_fusion.1
  50.2 1.6 gather_fusion.5
  51.8 4.3 %scatter_custom_fusion.4 = s32[2048]{0:T(1024)S(1)} fusion(s32[1024]{0:T(1024)S(1)} %broadcast_select_fusion, s32[1024]{0:T(1024)S(1)} %gather_fusion.3, s32[]{:T(128)} %constant.21.clone.1), kind=kCustom, calls=%fused_computation.82 | custom fusion | bytes 8196
  56.2 2.0 scatter_fusion
  58.2 0.1 copy.26
  58.3 21.2 %all_to_all.22 = s32[128,1,18]{2,1,0:T(1,128)S(1)} all-to-all(s32[128,1,18]{2,1,0:T(1,128)S(1)} %copy.26), channel_id=1, replica_groups=mesh['dp'=32,'mp'=4] {'dp','mp'}, dimensions={0} | all-to-all | bytes 18432 | tf_op jit(solution)/shard_map/all_to_all | solution.py:66
  79.5 0.1 reshape.253
  79.6 13.7 %gather_fusion.6 = bf16[2048,1024]{1,0:T(8,128)(2,1)} fusion(bf16[2048,1024]{1,0:T(8,128)(2,1)} %param.15, s32[2048]{0:T(1024)S(1)} %broadcast_clamp_fusion), kind=kCustom, calls=%fused_computation.6 | custom fusion | bytes 8396800 | tf_op jit(solution)/shard_map/gather | solution.py:67
  93.3 5.1 %all-to-all-start.1 = ((bf16[128,16,1024]{2,1,0:T(8,128)(2,1)}), bf16[128,16,1024]{2,1,0:T(8,128)(2,1)}, u32[]{:S(2)}, u32[]{:S(2)}) async-start(bf16[128,16,1024]{2,1,0:T(8,128)(2,1)} %bitcast.34), calls=%async_computation.1 | async-start | bytes 8388608 | tf_op jit(solution)/shard_map/all_to_all | solution.py:68
  98.5 0.1 reshape.186
  98.7 0.1 multiply_reduce_fusion.2
  98.8 0.1 and_reduce_fusion.1
  98.9 6.1 %scatter_custom_fusion.3 = f32[65536]{0:T(1024)S(1)} fusion(s32[1024]{0:T(1024)S(1)} %broadcast_select_fusion.1, f32[1024]{0:T(1024)S(1)} %reshape.289, f32[]{:T(128)} %constant.18.clone.1), kind=kCustom, calls=%fused_computation.50 | custom fusion | flops 1024 | bytes 262148
  105.1 45.9 %all_gather.6 = bf16[128,1024]{1,0:T(8,128)(2,1)S(1)} all-gather(bf16[32,1024]{1,0:T(8,128)(2,1)S(1)} %copy-done.4), channel_id=1, replica_groups=mesh['dp'=32,'mp'=4] {'mp'}, dimensions={0}, use_global_device_ids=true | all-gather | bytes 327680 | tf_op jit(solution)/shard_map/all_gather | solution.py:87
  151.0 0.1 fusion.16
  151.2 0.4 fusion.22
  151.5 0.5 all-to-all-done.1
  152.0 3.0 %fusion.14 = bf16[32,1024]{1,0:T(8,128)(2,1)S(1)} fusion(bf16[32,2048]{1,0:T(8,128)(2,1)S(1)} %reshape.200, bf16[2048,1024]{1,0:T(8,128)(2,1)} %bitcast.15, f32[32]{0:T(128)S(1)} %convert_element_type.59), kind=kOutput, calls=%fused_computation.30 | convolution fusion | flops 134283264 | bytes 4391040 | tf_op jit(solution)/shard_map/dot_general | solution.py:82
  155.1 10.0 %all_gather.7 = bf16[128,1024]{1,0:T(8,128)(2,1)S(1)} all-gather(bf16[32,1024]{1,0:T(8,128)(2,1)S(1)} %fusion.14), channel_id=1, replica_groups=mesh['dp'=32,'mp'=4] {'mp'}, dimensions={0}, use_global_device_ids=true | all-gather | bytes 327680 | tf_op jit(solution)/shard_map/all_gather | solution.py:88
  165.0 0.1 fusion.18
  165.2 2.7 %fusion.6 = f32[128,1280]{1,0:T(8,128)} fusion(bf16[512,256]{1,0:T(8,128)(2,1)S(1)} %copy-done.11, bf16[512,1024]{1,0:T(8,128)(2,1)} %param.27, f32[128,512]{1,0:T(8,128)S(1)} %fusion.22, bf16[1024,512]{1,0:T(8,128)(2,1)S(1)} %copy-done, bf16[128,1024]{1,0:T(8,128)(2,1)S(1)} %all_gather.7, f32[128]{0:T(128)S(1)} %add_rsqrt_fusion.1), kind=kOutput, calls=%fused_computation.20 | convolution fusion | flops 305201152 | bytes 3539456 | tf_op jit(solution)/shard_map/dot_general | solution.py:98
  168.1 0.1 slice_maximum_fusion
  168.2 0.1 reshape.261
  168.3 3.7 %gather_fusion.7 = bf16[256,256]{1,0:T(8,128)(2,1)S(1)} fusion(bf16[8192,256]{1,0:T(8,128)(2,1)} %param.24, s32[1024]{0:T(1024)S(1)} %pad_clamp_fusion), kind=kCustom, calls=%fused_computation.7 | custom fusion | bytes 263168 | tf_op jit(solution)/shard_map/gather | solution.py:120
  172.0 0.1 reshape.307
  172.2 20.8 %reduce-scatter.2.cloned.1.call-done = f32[32,1280]{1,0:T(8,128)} async-done(((f32[128,1280]{1,0:T(8,128)}), f32[32,1280]{1,0:T(8,128)}) %reduce-scatter.2.cloned.1.call-update) | async-done | bytes 163856 | tf_op jit(solution)/shard_map/reduce_scatter | solution.py:97
  192.9 5.6 %fusion.15 = bf16[32,1024]{1,0:T(8,128)(2,1)S(1)} fusion(bf16[2048,1024]{1,0:T(8,128)(2,1)} %bitcast.15, pred[32,2048]{1,0:T(32,128)(4,1)S(1)} %reshape.202, f32[32,1280]{1,0:T(8,128)} %reduce-scatter.2.cloned.1.call-done, f32[32]{0:T(128)S(1)} %convert_element_type.59), kind=kOutput, calls=%fused_computation.31 | convolution fusion | flops 268894208 | bytes 8585344 | tf_op jit(solution)/shard_map/dot_general | solution.py:109
  198.5 1.1 multiply_reduce_fusion
  199.7 0.7 broadcast_in_dim.70
  200.4 4.1 %scatter_fusion.1 = bf16[128,2,256]{2,1,0:T(2,128)(2,1)} fusion(bf16[128,2,256]{2,1,0:T(2,128)(2,1)} %broadcast_in_dim.70, s32[32]{0:T(128)S(1)} %fusion.40, bf16[32,256]{1,0:T(8,128)(2,1)S(1)} %multiply_convert_fusion), kind=kCustom, calls=%fused_computation.10 | custom fusion | bytes 49408 | tf_op jit(solution)/shard_map/scatter | solution.py:116
  204.5 9.2 %all-to-all-start.2 = ((bf16[128,2,256]{2,1,0:T(2,128)(2,1)}), bf16[128,2,256]{2,1,0:T(2,128)(2,1)S(1)}, u32[]{:S(2)}, u32[]{:S(2)}) async-start(bf16[128,2,256]{2,1,0:T(2,128)(2,1)} %scatter_fusion.1), calls=%async_computation.3 | async-start | bytes 262144 | tf_op jit(solution)/shard_map/all_to_all | solution.py:118
  213.8 0.1 slice_compare_fusion
  213.9 10.0 %all-to-all-done.2 = bf16[128,2,256]{2,1,0:T(2,128)(2,1)S(1)} async-done(((bf16[128,2,256]{2,1,0:T(2,128)(2,1)}), bf16[128,2,256]{2,1,0:T(2,128)(2,1)S(1)}, u32[]{:S(2)}, u32[]{:S(2)}) %all-to-all-start.2) | async-done | bytes 131104 | tf_op jit(solution)/shard_map/all_to_all | solution.py:118
  223.8 0.9 subtract_select_fusion
  (61 shorter events, 0.7 us)
Async XLA Ops:
  7.2 158.0 %copy-start = (bf16[1024,512]{1,0:T(8,128)(2,1)S(1)}, bf16[1024,512]{1,0:T(8,128)(2,1)}, u32[]{:S(2)}) copy-start(bf16[1024,512]{1,0:T(8,128)(2,1)} %param.26) | copy-start | bytes 3145732
  26.5 15.5 %copy-start.10 = (s32[2]{0:T(128)S(1)}, s32[2]{0:T(128)}, u32[]{:S(2)}) copy-start(s32[2]{0:T(128)} %constant.66) | copy-start | bytes 28
  26.5 15.6 %copy-start.9 = (s32[2]{0:T(128)S(1)}, s32[2]{0:T(128)}, u32[]{:S(2)}) copy-start(s32[2]{0:T(128)} %constant.69) | copy-start | bytes 28
  26.5 15.7 %copy-start.1 = (s32[262144]{0:T(1024)S(1)}, s32[262144]{0:T(1024)}, u32[]{:S(2)}) copy-start(s32[262144]{0:T(1024)} %param.20) | copy-start | bytes 3145732
  31.1 17.3 %copy-start.12 = (s32[32]{0:T(128)S(1)}, s32[32]{0:T(128)}, u32[]{:S(2)}) copy-start(s32[32]{0:T(128)} %param.21) | copy-start | bytes 388
  93.3 5.3 %copy-start.6 = (s32[32]{0:T(128)S(1)}, s32[32]{0:T(128)}, u32[]{:S(2)}) copy-start(s32[32]{0:T(128)} %param.18) | copy-start | bytes 388
  93.3 5.4 %copy-start.8 = (s32[2]{0:T(128)S(1)}, s32[2]{0:T(128)}, u32[]{:S(2)}) copy-start(s32[2]{0:T(128)} %constant.60) | copy-start | bytes 28
  93.3 5.5 %copy-start.7 = (s32[2]{0:T(128)S(1)}, s32[2]{0:T(128)}, u32[]{:S(2)}) copy-start(s32[2]{0:T(128)} %constant.63) | copy-start | bytes 28
  93.3 11.8 %copy-start.4 = (bf16[32,1024]{1,0:T(8,128)(2,1)S(1)}, bf16[32,1024]{1,0:T(8,128)(2,1)}, u32[]{:S(2)}) copy-start(bf16[32,1024]{1,0:T(8,128)(2,1)} %param.16) | copy-start | bytes 196612
  93.3 57.8 %copy-start.2 = (bf16[1024,512]{1,0:T(8,128)(2,1)S(1)}, bf16[1024,512]{1,0:T(8,128)(2,1)}, u32[]{:S(2)}) copy-start(bf16[1024,512]{1,0:T(8,128)(2,1)} %param.25) | copy-start | bytes 3145732
  93.3 58.7 %all-to-all-start.1 = ((bf16[128,16,1024]{2,1,0:T(8,128)(2,1)}), bf16[128,16,1024]{2,1,0:T(8,128)(2,1)}, u32[]{:S(2)}, u32[]{:S(2)}) async-start(bf16[128,16,1024]{2,1,0:T(8,128)(2,1)} %bitcast.34), calls=%async_computation.1 | async-start | bytes 8388608 | tf_op jit(solution)/shard_map/all_to_all | solution.py:68
  98.4 66.7 %copy-start.11 = (bf16[512,256]{1,0:T(8,128)(2,1)S(1)}, bf16[512,256]{1,0:T(8,128)(2,1)}, u32[]{:S(2)}) copy-start(bf16[512,256]{1,0:T(8,128)(2,1)} %param.28) | copy-start | bytes 786436
  98.4 94.5 %reduce-scatter.2.cloned.1.call-start = ((), (), s32[]{:S(2)}) async-start(), calls=%async_computation.4 | async-start | bytes 819200 | tf_op jit(solution)/shard_map/reduce_scatter | solution.py:97
  172.2 26.3 %copy-start.3 = (bf16[1024,256]{1,0:T(8,128)(2,1)S(1)}, bf16[1024,256]{1,0:T(8,128)(2,1)}, u32[]{:S(2)}) copy-start(bf16[1024,256]{1,0:T(8,128)(2,1)} %param.29) | copy-start | bytes 1572868
  199.6 25.1 %copy-start.5 = (bf16[32,256]{1,0:T(8,128)(2,1)}, bf16[32,256]{1,0:T(8,128)(2,1)S(1)}, u32[]{:S(2)}) copy-start(bf16[32,256]{1,0:T(8,128)(2,1)S(1)} %multiply_convert_fusion) | copy-start | bytes 49156
  204.5 19.3 %all-to-all-start.2 = ((bf16[128,2,256]{2,1,0:T(2,128)(2,1)}), bf16[128,2,256]{2,1,0:T(2,128)(2,1)S(1)}, u32[]{:S(2)}, u32[]{:S(2)}) async-start(bf16[128,2,256]{2,1,0:T(2,128)(2,1)} %scatter_fusion.1), calls=%async_computation.3 | async-start | bytes 262144 | tf_op jit(solution)/shard_map/all_to_all | solution.py:118
Sparse Core Ops, SparseCore 0:
  168.1 24.8 reduce-scatter.1
where the time goes:
time: 233 us; the launch traced here: 232 us
  blocking collectives  77.1 us (33%)
  local copies, waits for them, and re-layouts  68.6 us (29%)
  waiting for transfers between devices  31.2 us (13%)
  between operations  14.5 us (6%)
  starting transfers between devices  14.4 us (6%)
  other arithmetic  13.2 us (6%)
  matrix products  12.8 us (5%)
    all_gather x1, blocking collectives, local(): lax.all_gather(self_features, 'mp', axis=0, tiled=True)  45.9 us
    all_to_all x1, blocking collectives, local(): lax.all_to_all(requests, ('dp', 'mp'), split_axis=0, concat_axis=0, tiled...  21.2 us
    reduce_scatter x1, waiting for transfers between devices, local(): lax.psum_scatter(jnp.dot(hidden, w_both, preferred_element_type=jnp.float...  20.8 us
    gather x1, local copies, waits for them, and re-layouts, local(): lookups = features_table[incoming[:, :cap_fetch]]  13.7 us
    gather x1, local copies, waits for them, and re-layouts, local(): fetch_owner = node_owner[flat_ids]  13.4 us
    all_to_all x1, waiting for transfers between devices, local(): lax.all_to_all(outbound, ('dp', 'mp'), split_axis=0, concat_axis=0, tiled...  9.97 us
    all_gather x1, blocking collectives, local(): lax.all_gather(aggregate, 'mp', axis=0, tiled=True)  9.95 us
    all_to_all x1, starting transfers between devices, local(): lax.all_to_all(outbound, ('dp', 'mp'), split_axis=0, concat_axis=0, tiled...  9.24 us
  transfers between devices with their start and end apart: 3, of which 3 were waited for; matrix products, arithmetic and copies ran while one was open for 5% of the time, Pallas kernels for 0%

commit v1 on v0

v1 whole, which is shorter than its diff:
```python
import math

import jax
import jax.numpy as jnp
from jax import lax
from jax.experimental import pallas as pl
from jax.experimental.pallas import tpu as pltpu
from jax.sharding import PartitionSpec as P

MESH = pl.DeviceIdType.MESH
F32, BF16 = jnp.float32, jnp.bfloat16
STEP = 37


def dot(a, b):
    return jnp.dot(a, b, preferred_element_type=F32)


def dot_first(a, b):
    return lax.dot_general(a, b, (((0,), (0,)), ((), ())), preferred_element_type=F32)


def rms_rows(values):
    return values * lax.rsqrt(jnp.mean(values * values, axis=-1, keepdims=True) + 1e-06)


def iota(shape, dim):
    return lax.broadcasted_iota(jnp.int32, shape, dim)


def pick(mask, values):
    return jnp.sum(jnp.where(mask, values, 0.0), axis=1, keepdims=True)


def one_hot(mask):
    return jnp.where(mask, 1.0, 0.0).astype(BF16)


def split16(values):
    high = jnp.floor(values * (1.0 / 128.0)) * 128.0
    return high.astype(BF16), (values - high).astype(BF16)


def offset(i):
    k = lax.rem(i * STEP, 128)
    return lax.rem(k, 4), lax.rem(lax.div(k, 4), 2), lax.rem(lax.div(k, 8), 4), lax.div(k, 32)


def kernel(
    ids, cnt, lids_s, lids, self_f, node_owner, node_row, list_owner, list_row, features, centroids,
    w_self, w_neigh, w_query, w_out, w_context,
    emb_out, res_out,
    no_v, nr_v, lo_v, lr_v, ft, ct, ws, wn, wq, wo, wc,
    btab, rq, ra, rbs, rb, rhi, rlo, lo_rows, lr_rows, sb, gb, plb, obt, ns, na, s1, ps, pr, cen, obuf, ea, ebs, eb,
    load_sem, send_sem, recv_sem, row_sem,
):
    dp, x = lax.axis_index("dp"), lax.axis_index("mp")
    c, yz = lax.rem(dp, 2), lax.div(dp, 2)
    z, y = lax.rem(yz, 4), lax.div(yz, 4)
    cx = c * 4 + x

    loads = [
        pltpu.make_async_copy(src, dst, load_sem.at[i])
        for i, (src, dst) in enumerate(
            [(node_owner, no_v), (node_row, nr_v), (list_owner, lo_v), (list_row, lr_v), (features, ft), (w_self, ws),
             (centroids, ct), (w_neigh, wn), (w_query, wq), (w_out, wo), (w_context, wc)]
        )
    ]
    for load in loads:
        load.start()

    barrier = pltpu.get_barrier_semaphore()

    def yz_peer(i):
        return lax.rem(yz + i, 16)

    def cx_peer(i):
        return lax.rem(cx + i, 8)

    def greet_yz(i, _):
        pl.semaphore_signal(barrier, inc=1, device_id=(yz_peer(i) * 2 + c, x), device_id_type=MESH)
        return 0

    def greet_cx(i, _):
        p = cx_peer(i)
        pl.semaphore_signal(barrier, inc=1, device_id=(yz * 2 + lax.div(p, 4), lax.rem(p, 4)), device_id_type=MESH)
        return 0

    lax.fori_loop(1, 16, greet_yz, 0)
    lax.fori_loop(1, 8, greet_cx, 0)

    def remote(src, dst, which, device, recv=None):
        return pltpu.make_async_remote_copy(
            src_ref=src, dst_ref=dst, send_sem=send_sem.at[which], recv_sem=recv_sem.at[which] if recv is None else recv,
            device_id=device, device_id_type=MESH,
        )

    def landed(ref, sem):
        pltpu.make_async_copy(ref, ref, sem).wait()

    ns[pl.ds(0, 32), :] = rms_rows(self_f[...].astype(F32)).astype(BF16)

    loads[0].wait()
    loads[1].wait()
    btab[:, 0:128] = no_v[...].astype(F32).astype(BF16)
    rows_f = nr_v[...]
    btab[:, 128:256] = lax.shift_left(lax.shift_right_logical(rows_f, 4), 4).astype(F32).astype(BF16)
    btab[:, 256:384] = jnp.bitwise_and(rows_f, 15).astype(F32).astype(BF16)
    ids_all = ids[...]
    lane = iota((256, 128), 1)
    tri = one_hot(iota((256, 256), 1) < iota((256, 256), 0))
    carry = jnp.zeros((1, 128), F32)
    slot_row = iota((256, 1), 0)
    node = (lax.rem(slot_row, 32) + 1).astype(F32)
    counts8 = jnp.concatenate([cnt[...]] * 8, axis=0)
    request = jnp.zeros((128, 128), F32)
    for q in range(4):
        idc = jnp.concatenate([ids_all[:, 8 * q + j : 8 * q + j + 1] for j in range(8)], axis=0)
        found = dot(one_hot(iota((256, 2048), 1) == lax.shift_right_logical(idc, 7)), btab[...])
        sel = lane == jnp.bitwise_and(idc, 127)
        owner = pick(sel, found[:, 0:128])
        high, low = pick(sel, found[:, 128:256]), pick(sel, found[:, 256:384])
        mine = lane.astype(F32) == owner
        hot = one_hot(mine)
        rank = pick(mine, dot(tri, hot) + carry)
        carry = carry + jnp.sum(jnp.where(mine, 1.0, 0.0), axis=0, keepdims=True)
        valid = (lax.div(slot_row, 32) + 8 * q) < counts8
        here = lane.astype(F32) == rank
        there = (lane - 32).astype(F32) == rank
        x_high = jnp.where(here, high, jnp.where(there, jnp.where(valid, node, 0.0), 0.0)).astype(BF16)
        x_low = jnp.where(here, low, 0.0).astype(BF16)
        request = request + dot_first(hot, x_high) + dot_first(hot, x_low)

    loads[2].wait()
    loads[3].wait()

    def list_lookup(n, _):
        r = lax.div(lids_s[n], 128)
        lo_rows[pl.ds(n, 1), :] = lo_v[pl.ds(r, 1), :]
        lr_rows[pl.ds(n, 1), :] = lr_v[pl.ds(r, 1), :]
        return 0

    lax.fori_loop(0, 32, list_lookup, 0, unroll=8)
    lane32 = iota((32, 128), 1)
    lsel = lane32 == jnp.bitwise_and(lids[...], 127)
    dest = pick(lsel, lo_rows[...].astype(F32))
    lrow = pick(lsel, lr_rows[...].astype(F32)) + 1.0
    lmine = lane32.astype(F32) == dest
    lhot = one_hot(lmine)
    lrank = pick(lmine, dot(one_hot(iota((32, 32), 1) < iota((32, 32), 0)), lhot))
    lhigh, llow = split16(lrow)
    lthere = (lane32 - 16).astype(F32) == lrank
    request = request + dot_first(lhot, jnp.where(lthere, lhigh.astype(F32), 0.0).astype(BF16))
    request = request + dot_first(lhot, jnp.where(lthere, llow.astype(F32), 0.0).astype(BF16))
    obt[...] = one_hot(iota((32, 256), 1).astype(F32) == dest * 2.0 + lrank)
    rq[...] = request

    pl.semaphore_wait(barrier, 22)

    def ask_yz(i, _):
        p = yz_peer(i)
        remote(rq.at[pl.ds(pl.multiple_of(p * 8, 8), 8), :], ra.at[pl.ds(pl.multiple_of(yz * 8, 8), 8), :], 0, (p * 2 + c, x)).start()
        return 0

    lax.fori_loop(1, 16, ask_yz, 0)
    own = pl.ds(pl.multiple_of(yz * 8, 8), 8)
    ra[own, :] = rq[own, :]
    landed(ra.at[pl.ds(0, 120), :], recv_sem.at[0])
    for p in range(8):
        rbs[pl.ds(16 * p, 16), :] = ra[pl.ds(p, 16, stride=8), :]

    def ask_cx(i, _):
        p = cx_peer(i)
        remote(rbs.at[pl.ds(pl.multiple_of(p * 16, 16), 16), :], rb.at[pl.ds(pl.multiple_of(cx * 16, 16), 16), :], 1, (yz * 2 + lax.div(p, 4), lax.rem(p, 4))).start()
        return 0

    lax.fori_loop(1, 8, ask_cx, 0)
    own = pl.ds(pl.multiple_of(cx * 16, 16), 16)
    rb[own, :] = rbs[own, :]

    for i in range(1, 4):
        remote(ns.at[pl.ds(0, 32), :], ns.at[pl.ds(32 * i, 32), :], 2, (dp, lax.rem(x + i, 4))).start()

    order_row, order_lane = iota((128, 128), 0), iota((128, 128), 1)
    kx, kc, kz, ky = offset(order_row)
    from_owner = (lax.rem(y + 4 - ky, 4) * 4 + lax.rem(z + 4 - kz, 4)) * 8 + lax.rem(c + kc, 2) * 4 + lax.rem(x + 4 - kx, 4)
    to_asker = (lax.rem(c + kc, 2) * 4 + lax.rem(x + kx, 4)) * 16 + lax.rem(y + ky, 4) * 4 + lax.rem(z + kz, 4)
    spread = one_hot(lax.div(iota((256, 16), 0), 16) == iota((256, 16), 1))
    sub = lax.rem(iota((256, 128), 0), 16)
    nodes = dot(one_hot(order_lane == from_owner), split16(request)[1]).astype(BF16)
    for g in range(8):
        held = pick(lane == sub + 32, dot(spread, nodes[16 * g : 16 * g + 16, :]))
        member = jnp.where((lane + 1).astype(F32) == held, 1.0, 0.0)
        plb[:, 256 * g : 256 * g + 256] = jnp.transpose(member)[0:32, :].astype(BF16)

    loads[4].wait()
    landed(rb.at[pl.ds(0, 112), :], recv_sem.at[1])

    asker = one_hot(order_lane == to_asker)
    asked_high, asked_low = split16(rb[...])
    rhi[...] = dot(asker, asked_high)
    rlo[...] = dot(asker, asked_low)

    def serve(g, _):
        block = pl.ds(pl.multiple_of(16 * g, 16), 16)
        asked = dot(spread, rhi[block, :].astype(BF16)) + dot(spread, rlo[block, :].astype(BF16))
        index = pick(lane == sub, asked).astype(jnp.int32)
        rows = dot(one_hot(iota((256, 2048), 1) == index), ft[...]).astype(BF16)
        sb[pl.ds(pl.multiple_of(256 * g, 256), 256), :] = rows

        def send(j, _):
            i = 16 * g + j
            kx, kc, kz, ky = offset(i)
            device = ((lax.rem(y + ky, 4) * 4 + lax.rem(z + kz, 4)) * 2 + lax.rem(c + kc, 2), lax.rem(x + kx, 4))
            part = pl.ds(pl.multiple_of(16 * i, 16), 16)
            remote(sb.at[part, :], gb.at[part, :], 3, device, row_sem.at[g]).start()
            return 0

        lax.fori_loop(jnp.where(g == 0, 1, 0), 16, send, 0)
        return 0

    lax.fori_loop(0, 8, serve, 0)
    gb[pl.ds(0, 16), :] = sb[pl.ds(0, 16), :]

    landed(ns.at[pl.ds(32, 96), :], recv_sem.at[2])
    loads[5].wait()
    s1[...] = dot(ns[...], ws[...])
    loads[6].wait()
    lists = jnp.concatenate([rb[pl.ds(p, 8, stride=16), :] for p in range(16)], axis=0)
    wanted = jnp.concatenate([lists[:, 16:17], lists[:, 17:18]], axis=0)
    wanted_i = wanted.astype(jnp.int32) - 1

    def centre(k, total):
        hot = one_hot(iota((256, 1024), 1) + 1024 * k == wanted_i)
        return total + dot(hot, ct[pl.ds(pl.multiple_of(1024 * k, 1024), 1024), :])

    cen[...] = lax.fori_loop(0, 8, centre, jnp.zeros((256, 256), F32))

    total = jnp.zeros((32, 1024), F32)
    for g in range(8):
        first = 16 if g == 0 else 0
        landed(gb.at[pl.ds(256 * g + first, 256 - first), :], row_sem.at[g])
        total = total + dot(plb[:, 256 * g : 256 * g + 256], gb[pl.ds(256 * g, 256), :])
    counts = cnt[...].astype(F32)
    aggregate = (total / counts).astype(BF16)
    na[pl.ds(0, 32), :] = rms_rows(aggregate.astype(F32)).astype(BF16)
    for i in range(1, 4):
        remote(na.at[pl.ds(0, 32), :], na.at[pl.ds(32 * i, 32), :], 4, (dp, lax.rem(x + i, 4))).start()
    for load in loads[7:]:
        load.wait()
    landed(na.at[pl.ds(32, 96), :], recv_sem.at[4])
    hidden = jnp.maximum(s1[...] + dot(na[...], wn[...]), 0.0).astype(BF16)
    ps[:, 0:1024] = dot(hidden, wq[...])
    ps[:, 1024:1280] = dot(hidden, wo[...])
    for i in range(1, 4):
        part = pl.ds(32 * i, 32)
        remote(ps.at[part, :], pr.at[part, :], 5, (dp, lax.rem(x + 4 - i, 4))).start()
    pr[pl.ds(0, 32), :] = ps[pl.ds(0, 32), :]
    landed(pr.at[pl.ds(32, 96), :], recv_sem.at[5])
    terms = (pr[pl.ds(0, 32), :] + pr[pl.ds(32, 32), :]) + (pr[pl.ds(64, 32), :] + pr[pl.ds(96, 32), :])
    queries = terms[:, 0:1024].astype(BF16)
    scores = lax.dot_general(queries, gb[...], (((1,), (1,)), ((), ())), preferred_element_type=F32)
    gates = jnp.where(plb[...].astype(F32) > 0.5, jax.nn.sigmoid(scores * (1.0 / 32.0)), 0.0).astype(BF16)
    context = (dot(gates, gb[...]) / counts).astype(BF16)
    embedding = rms_rows(terms[:, 1024:1280] + dot(context, wc[...])).astype(BF16)
    emb_out[...] = embedding

    obuf[...] = dot_first(obt[...], embedding).astype(BF16)

    def tell_yz(i, _):
        p = yz_peer(i)
        remote(obuf.at[pl.ds(pl.multiple_of(p * 16, 16), 16), :], ea.at[pl.ds(pl.multiple_of(yz * 16, 16), 16), :], 6, (p * 2 + c, x)).start()
        return 0

    lax.fori_loop(1, 16, tell_yz, 0)
    own = pl.ds(pl.multiple_of(yz * 16, 16), 16)
    ea[own, :] = obuf[own, :]
    r0, r1 = iota((256, 256), 0), iota((256, 256), 1)
    turn = one_hot(r1 == lax.rem(r0, 16) * 16 + lax.div(r0, 32) * 2 + lax.rem(lax.div(r0, 16), 2))
    back = one_hot(r1 == lax.rem(r0, 8) * 32 + lax.div(r0, 128) * 16 + lax.rem(lax.div(r0, 8), 16))
    landed(ea.at[pl.ds(0, 240), :], recv_sem.at[6])
    ebs[...] = dot(turn, ea[...]).astype(BF16)

    def tell_cx(i, _):
        p = cx_peer(i)
        remote(ebs.at[pl.ds(pl.multiple_of(p * 32, 32), 32), :], eb.at[pl.ds(pl.multiple_of(cx * 32, 32), 32), :], 7, (yz * 2 + lax.div(p, 4), lax.rem(p, 4))).start()
        return 0

    lax.fori_loop(1, 8, tell_cx, 0)
    own = pl.ds(pl.multiple_of(cx * 32, 32), 32)
    eb[own, :] = ebs[own, :]
    landed(eb.at[pl.ds(0, 224), :], recv_sem.at[7])
    arrived = dot(back, eb[...])
    res_out[...] = jnp.where(wanted > 0.5, arrived - cen[...], 0.0)

    landed(rq.at[pl.ds(0, 120), :], send_sem.at[0])
    landed(rbs.at[pl.ds(0, 112), :], send_sem.at[1])
    landed(ns.at[pl.ds(0, 96), :], send_sem.at[2])
    landed(sb.at[pl.ds(16, 2032), :], send_sem.at[3])
    landed(na.at[pl.ds(0, 96), :], send_sem.at[4])
    landed(ps.at[pl.ds(32, 96), :], send_sem.at[5])
    landed(obuf.at[pl.ds(0, 240), :], send_sem.at[6])
    landed(ebs.at[pl.ds(0, 224), :], send_sem.at[7])


def local(
    features_table, self_features, neighbour_ids, neighbour_counts, node_owner, node_row, list_ids, list_owner,
    list_row, centroids, w_self, w_neigh, w_query, w_out, w_context,
):
    vmem, smem, anyw = (pl.BlockSpec(memory_space=m) for m in (pltpu.VMEM, pltpu.SMEM, pl.ANY))
    i32 = jnp.int32
    scratch = [
        ((2048, 128), i32), ((2048, 128), i32), ((8192, 128), i32), ((8192, 128), i32), ((2048, 1024), BF16),
        ((8192, 256), BF16), ((1024, 512), BF16), ((1024, 512), BF16), ((512, 1024), BF16), ((512, 256), BF16),
        ((1024, 256), BF16),
        ((2048, 384), BF16), ((128, 128), F32), ((128, 128), F32), ((128, 128), F32), ((128, 128), F32),
        ((128, 128), F32), ((128, 128), F32), ((32, 128), i32), ((32, 128), i32),
        ((2048, 1024), BF16), ((2048, 1024), BF16), ((32, 2048), BF16), ((32, 256), BF16), ((128, 1024), BF16),
        ((128, 1024), BF16), ((128, 512), F32), ((128, 1280), F32), ((128, 1280), F32), ((256, 256), F32),
        ((256, 256), BF16), ((256, 256), BF16), ((256, 256), BF16), ((256, 256), BF16),
    ]
    embedding, residual = pl.pallas_call(
        kernel,
        out_shape=(jax.ShapeDtypeStruct((32, 256), BF16), jax.ShapeDtypeStruct((256, 256), F32)),
        in_specs=[vmem, vmem, smem, vmem, vmem] + [anyw] * 11,
        out_specs=(vmem, vmem),
        scratch_shapes=[pltpu.VMEM(s, t) for s, t in scratch]
        + [pltpu.SemaphoreType.DMA((11,)), pltpu.SemaphoreType.DMA((8,)), pltpu.SemaphoreType.DMA((8,)), pltpu.SemaphoreType.DMA((8,))],
        compiler_params=pltpu.CompilerParams(collective_id=0, has_side_effects=True, vmem_limit_bytes=56 << 20),
    )(
        neighbour_ids, neighbour_counts.reshape(32, 1), list_ids, list_ids.reshape(32, 1), self_features,
        node_owner.reshape(2048, 128), node_row.reshape(2048, 128), list_owner.reshape(8192, 128),
        list_row.reshape(8192, 128), features_table, centroids, w_self, w_neigh, w_query, w_out, w_context,
    )
    return embedding, residual.reshape(2, 128, 256).transpose(1, 0, 2)


def solution(mesh):
    placed = (
        P(("dp", "mp"), None),
        P(("dp", "mp"), None),
        P(("dp", "mp"), None),
        P(("dp", "mp")),
        P(),
        P(),
        P(("dp", "mp")),
        P(),
        P(),
        P(("dp", "mp"), None),
        P(None, "mp"),
        P(None, "mp"),
        P("mp", None),
        P("mp", None),
        P(),
    )
    return jax.shard_map(
        local,
        mesh=mesh,
        in_specs=placed,
        out_specs=(P(("dp", "mp"), None), P(("dp", "mp"), None, None)),
        check_vma=False,
    )
```

time: 233 us -> 107 us (0.46)
  Pallas kernels: 0 us -> 99.7 us
  blocking collectives: 77.1 us -> 0 us
  local copies, waits for them, and re-layouts: 68.6 us -> 5.86 us
  waiting for transfers between devices: 31.2 us -> 0 us
  starting transfers between devices: 14.4 us -> 0 us
  between operations: 14.5 us -> 0.64 us
  other arithmetic: 13.2 us -> 0 us
  matrix products: 12.8 us -> 0 us
    pallas_call x0 -> x1, Pallas kernels: none -> 99.7 us  [local(): pl.pallas_call(kernel, out_shape=(jax.ShapeDtypeStruct((32, 256), BF16),...]
    all_gather x2 -> x0, blocking collectives: 55.9 us -> none  [the longest x1 45.9 us: local(): lax.all_gather(self_features, 'mp', axis=0, tiled=True)]
    gather x8 -> x0, local copies, waits for them, and re-layouts: 51.3 us -> none  [the longest x1 13.7 us: local(): lookups = features_table[incoming[:, :cap_fetch]]]
    all_to_all x1 -> x0, blocking collectives: 21.2 us -> none  [local(): lax.all_to_all(requests, ('dp', 'mp'), split_axis=0, concat_axis=0, tiled...]
    reduce_scatter x1 -> x0, waiting for transfers between devices: 20.8 us -> none  [local(): lax.psum_scatter(jnp.dot(hidden, w_both, preferred_element_type=jnp.float...]
    all_to_all x2 -> x0, starting transfers between devices: 14.3 us -> none  [the longest x1 9.24 us: local(): lax.all_to_all(outbound, ('dp', 'mp'), split_axis=0, concat_axis=0, tiled...]
    dot_general x5 -> x0, matrix products: 12.8 us -> none  [the longest x1 5.57 us: local(): gated_sums = jnp.dot(gates, returned, preferred_element_type=jnp.float32)]
    all_to_all x2 -> x0, waiting for transfers between devices: 10.5 us -> none  [the longest x1 9.97 us: local(): lax.all_to_all(outbound, ('dp', 'mp'), split_axis=0, concat_axis=0, tiled...]
  transfers between devices with their start and end apart: 3 -> 0, of which waited for: 3 -> 0; matrix products, arithmetic and copies ran while one was open for 5% -> 0% of each run, Pallas kernels for 0% -> 0%
where the time goes in v1:
time: 107 us; the launch traced here: 106 us
  Pallas kernels  99.7 us (93%)
  local copies, waits for them, and re-layouts  5.86 us (5%)
    pallas_call x1, Pallas kernels, local(): pl.pallas_call(kernel, out_shape=(jax.ShapeDtypeStruct((32, 256), BF16),...  99.7 us

profile of v1, /device:TPU:1, one launch (start us, length us, event | category | flops | bytes accessed | tf_op | source)
XLA Modules:
  0.0 106.2 jit_solution(11005295220781117428)
XLA Ops:
  0.6 1.3 %copy.17.cnt = s32[32,1]{1,0:T(8,128)} copy(s32[32,1]{0,1:T(1,128)} %bitcast.17) | data formatting | bytes 256 | tf_op jit(solution)/shard_map/reshape | solution.py:331
  2.0 1.3 %copy.18.lids = s32[32,1]{1,0:T(8,128)} copy(s32[32,1]{0,1:T(1,128)} %bitcast.16) | data formatting | bytes 256 | tf_op jit(solution)/shard_map/reshape | solution.py:331
  3.3 99.7 %shard_map.158 = (bf16[32,256]{1,0:T(8,128)(2,1)}, f32[256,256]{1,0:T(8,128)}) custom-call(s32[32,32]{1,0:T(8,128)} %ids.1, s32[32,1]{1,0:T(8,128)} %copy.17.cnt, s32[32]{0:T(128)} %lids_s.1, s32[32,1]{1,0:T(8,128)} %copy.18.lids, bf16[32,1024]{1,0:T(8,128)(2,1)} %self_f.1, s32[2048,128]{1,0:T(8,128)} %bitcast.12, s32[2048,128]{1,0:T(8,128)} %bitcast.13, ...), custom_call_target="tpu_custom_call" | custom-call | tf_op jit(solution)/shard_map/pallas_call | solution.py:322
  103.1 1.9 %copy.21 = f32[2,128,256]{2,0,1:T(2,128)} copy(f32[2,128,256]{2,1,0:T(8,128)} %bitcast.15) | data formatting | bytes 524288 | tf_op jit(solution)/shard_map/reshape | solution.py:335
  104.9 1.3 %copy.23 = bf16[32,256]{1,0:T(8,128)(2,1)} copy(bf16[32,256]{1,0:T(8,128)(2,1)} %get-tuple-element.8) | data formatting | bytes 32768

commit v2 on v1

v2 whole, which is shorter than its diff:
```python
import math

import jax
import jax.numpy as jnp
from jax import lax
from jax.experimental import pallas as pl
from jax.experimental.pallas import tpu as pltpu
from jax.sharding import PartitionSpec as P

MESH = pl.DeviceIdType.MESH
F32, BF16 = jnp.float32, jnp.bfloat16


def dot(a, b):
    return jnp.dot(a, b, preferred_element_type=F32)


def dot_first(a, b):
    return lax.dot_general(a, b, (((0,), (0,)), ((), ())), preferred_element_type=F32)


def rms_rows(values):
    return values * lax.rsqrt(jnp.mean(values * values, axis=-1, keepdims=True) + 1e-06)


def iota(shape, dim):
    return lax.broadcasted_iota(jnp.int32, shape, dim)


def pick(mask, values):
    return jnp.sum(jnp.where(mask, values, 0.0), axis=1, keepdims=True)


def spread_pick(mask, values, ones):
    return dot(jnp.where(mask, values, 0.0).astype(BF16), ones)


def column(row):
    return jnp.sum(jnp.where(iota((32, 32), 0) == iota((32, 32), 1), row.astype(F32), 0.0), axis=1, keepdims=True)


def one_hot(mask):
    return jnp.where(mask, 1.0, 0.0).astype(BF16)


def split16(values):
    high = jnp.floor(values * (1.0 / 128.0)) * 128.0
    return high.astype(BF16), (values - high).astype(BF16)


def offset(i):
    g, a, b = lax.div(i, 16), lax.div(lax.rem(i, 16), 4), lax.rem(i, 4)
    return b, lax.rem(lax.div(g, 4) + a + lax.div(b, 2), 2), lax.rem(a + b, 4), lax.rem(g + a + 3 * b, 4)


def kernel(
    ids, cnt, lids_s, lids, self_f, node_owner, node_row, list_owner, list_row, features, centroids,
    w_self, w_neigh, w_query, w_out, w_context,
    emb_out, eb, cen,
    no_v, nr_v, lo_v, lr_v, ft, ct, ws, wn, wq, wo, wc,
    btab, rq, rb, held, lo_rows, lr_rows, sb, gb, plb, obt, ns, na, s1, ps, pr, ob, load_sem, send_sem, recv_sem, ask_sem, row_sem,
):
    dp, x = lax.axis_index("dp"), lax.axis_index("mp")
    c, yz = lax.rem(dp, 2), lax.div(dp, 2)
    z, y = lax.rem(yz, 4), lax.div(yz, 4)
    me = dp * 4 + x

    def partners(g, sign):
        xs = [lax.rem(x + (sign * k) % 4, 4) for k in range(4)]
        zs = [lax.rem(z + (sign * k) % 4, 4) * 2 for k in range(4)]
        ys = [lax.rem(y + 16 + sign * (g + k), 4) * 8 for k in range(4)]
        cs = [lax.rem(c + lax.div(g, 4) + k, 2) for k in range(2)]
        return [
            (ys[(j // 4 + 3 * (j % 4)) % 4] + zs[(j // 4 + j % 4) % 4] + cs[(j // 4 + j % 4 // 2) % 2], xs[j % 4])
            for j in range(16)
        ]

    loads = [
        pltpu.make_async_copy(src, dst, load_sem.at[i])
        for i, (src, dst) in enumerate(
            [(node_owner, no_v), (node_row, nr_v), (list_owner, lo_v), (list_row, lr_v), (features, ft), (w_self, ws),
             (centroids, ct), (w_neigh, wn), (w_query, wq), (w_out, wo), (w_context, wc)]
        )
    ]
    for load in loads:
        load.start()

    barrier = pltpu.get_barrier_semaphore()

    def greet(j_first):
        def body(g, _):
            for device in partners(g, 1)[j_first:]:
                pl.semaphore_signal(barrier, inc=1, device_id=device, device_id_type=MESH)
            return 0

        return body

    greet(1)(jnp.int32(0), 0)
    lax.fori_loop(1, 8, greet(0), 0)

    def remote(src, dst, which, device, recv=None):
        return pltpu.make_async_remote_copy(
            src_ref=src, dst_ref=dst, send_sem=send_sem.at[which], recv_sem=recv_sem.at[which] if recv is None else recv,
            device_id=device, device_id_type=MESH,
        )

    def landed(ref, sem):
        pltpu.make_async_copy(ref, ref, sem).wait()

    ns[pl.ds(0, 32), :] = rms_rows(self_f[...].astype(F32)).astype(BF16)

    loads[0].wait()
    loads[1].wait()
    code = no_v[...] * 2048 + nr_v[...]
    btab[:, 0:128] = (lax.shift_right_logical(code, 9) - 256).astype(F32).astype(BF16)
    btab[:, 128:256] = (jnp.bitwise_and(code, 511) - 256).astype(F32).astype(BF16)
    ones = jnp.ones((128, 128), BF16)
    counts = column(cnt[...])
    ids_all = ids[...]
    lane = iota((256, 128), 1)
    lane_f = lane.astype(F32)
    tri = one_hot(iota((256, 256), 1) < iota((256, 256), 0))
    carry = jnp.zeros((1, 128), F32)
    slot_row = iota((256, 1), 0)
    node = (lax.rem(slot_row, 32) + 1).astype(F32)
    counts8 = jnp.concatenate([counts] * 8, axis=0)
    request = jnp.zeros((128, 128), F32)
    for q in range(4):
        idc = jnp.concatenate([ids_all[:, 8 * q + j : 8 * q + j + 1] for j in range(8)], axis=0)
        found = dot(one_hot(iota((256, 2048), 1) == lax.shift_right_logical(idc, 7)), btab[...])
        sel = lane == jnp.bitwise_and(idc, 127)
        code = (spread_pick(sel, found[:, 0:128], ones) + 256.0) * 512.0 + (spread_pick(sel, found[:, 128:256], ones) + 256.0)
        owner = jnp.floor(code * (1.0 / 2048.0))
        row = code - owner * 2048.0
        high = jnp.floor(row * (1.0 / 16.0)) * 16.0
        low = row - high
        mine = lane_f == owner
        hot = one_hot(mine)
        rank = spread_pick(mine, dot(tri, hot) + carry, ones)
        carry = carry + jnp.sum(jnp.where(mine, 1.0, 0.0), axis=0, keepdims=True)
        valid = (lax.div(slot_row, 32) + 8 * q).astype(F32) < counts8
        here = lane_f == rank
        there = lane_f - 32.0 == rank
        x_high = jnp.where(here, high, jnp.where(there, jnp.where(valid, node, 0.0), 0.0)).astype(BF16)
        x_low = jnp.where(here, low, 0.0).astype(BF16)
        request = request + dot_first(hot, x_high) + dot_first(hot, x_low)

    loads[2].wait()
    loads[3].wait()

    def list_lookup(n, _):
        r = lax.div(lids_s[n], 128)
        lo_rows[pl.ds(n, 1), :] = lo_v[pl.ds(r, 1), :]
        lr_rows[pl.ds(n, 1), :] = lr_v[pl.ds(r, 1), :]
        return 0

    lax.fori_loop(0, 32, list_lookup, 0, unroll=8)
    lane32 = iota((32, 128), 1)
    lsel = lane32 == column(jnp.bitwise_and(lids[...], 127)).astype(jnp.int32)
    dest = pick(lsel, lo_rows[...].astype(F32))
    lrow = pick(lsel, lr_rows[...].astype(F32)) + 1.0
    lmine = lane32.astype(F32) == dest
    lhot = one_hot(lmine)
    lrank = pick(lmine, dot(one_hot(iota((32, 32), 1) < iota((32, 32), 0)), lhot))
    lhigh, llow = split16(lrow)
    lthere = (lane32 - 16).astype(F32) == lrank
    request = request + dot_first(lhot, jnp.where(lthere, lhigh.astype(F32), 0.0).astype(BF16))
    request = request + dot_first(lhot, jnp.where(lthere, llow.astype(F32), 0.0).astype(BF16))
    obt[...] = one_hot(iota((32, 256), 1).astype(F32) == dest + 128.0 * lrank)

    order_row, order_lane = iota((128, 128), 0), iota((128, 128), 1)
    kx, kc, kz, ky = offset(order_row)
    from_dp = (lax.rem(y + 4 - ky, 4) * 4 + lax.rem(z + 4 - kz, 4)) * 2 + lax.rem(c + kc, 2)
    asked = one_hot(order_lane == from_dp * 4 + lax.rem(x + 4 - kx, 4))
    high, low = split16(request)
    low = dot(asked, low)
    held[...] = low.astype(BF16)
    rq[:, 0, :] = dot(asked, high) + low

    pl.semaphore_wait(barrier, 127)

    def ask(j_first):
        def body(g, _):
            for j, device in list(enumerate(partners(g, -1)))[j_first:]:
                i = 16 * g + j
                remote(rq.at[i], rb.at[i], 0, device, ask_sem.at[g]).start()
            return 0

        return body

    pltpu.make_async_copy(rq.at[0], rb.at[0], ask_sem.at[0]).start()
    ask(1)(0, 0)
    lax.fori_loop(1, 8, ask(0), 0)

    for i in range(1, 4):
        remote(ns.at[pl.ds(0, 32), :], ns.at[pl.ds(32 * i, 32), :], 2, (dp, lax.rem(x + i, 4))).start()

    spread = one_hot(lax.div(iota((256, 16), 0), 16) == iota((256, 16), 1))
    sub = lax.rem(iota((256, 128), 0), 16)
    loads[4].wait()

    def serve(j_first):
        def body(g, _):
            block = pl.ds(pl.multiple_of(16 * g, 16), 16)
            landed(rb.at[block], ask_sem.at[g])
            high, low = split16(rb[block, 0, :])
            index = pick(lane == sub, dot(spread, high) + dot(spread, low)).astype(jnp.int32)
            rows = dot(one_hot(iota((256, 2048), 1) == index), ft[...]).astype(BF16)
            sb[pl.ds(pl.multiple_of(256 * g, 256), 256), :] = rows
            for j, device in list(enumerate(partners(g, 1)))[j_first:]:
                part = pl.ds(pl.multiple_of(256 * g + 16 * j, 16), 16)
                remote(sb.at[part, :], gb.at[part, :], 3, device, row_sem.at[g]).start()
            return 0

        return body

    serve(1)(0, 0)
    own_rows = pltpu.make_async_copy(sb.at[pl.ds(0, 16), :], gb.at[pl.ds(0, 16), :], row_sem.at[0])
    own_rows.start()
    lax.fori_loop(1, 8, serve(0), 0)

    for g in range(8):
        node = pick(lane == sub + 32, dot(spread, held[pl.ds(16 * g, 16), :]))
        member = jnp.where(lane_f + 1.0 == node, 1.0, 0.0)
        plb[:, 256 * g : 256 * g + 256] = jnp.transpose(member)[0:32, :].astype(BF16)


    landed(ns.at[pl.ds(32, 96), :], recv_sem.at[2])
    loads[5].wait()
    s1[...] = dot(ns[...], ws[...])
    loads[6].wait()
    kx, kc, kz, ky = offset(order_lane)
    to_dp = (lax.rem(y + ky, 4) * 4 + lax.rem(z + kz, 4)) * 2 + lax.rem(c + kc, 2)
    by_source = one_hot(order_row == to_dp * 4 + lax.rem(x + kx, 4))
    high, low = split16(rb[:, 0, :])
    lists = dot(by_source, high) + dot(by_source, low)
    wanted = jnp.concatenate([lists[:, 16:17], lists[:, 17:18]], axis=0).astype(jnp.int32) - 1

    def centre(k, total):
        hot = one_hot(iota((256, 1024), 1) + 1024 * k == wanted)
        return total + dot(hot, ct[pl.ds(pl.multiple_of(1024 * k, 1024), 1024), :])

    centres = lax.fori_loop(0, 8, centre, jnp.zeros((256, 256), F32))
    cen[:, 0, :] = centres[0:128, :]
    cen[:, 1, :] = centres[128:256, :]

    total = jnp.zeros((32, 1024), F32)
    for g in range(8):
        landed(gb.at[pl.ds(256 * g, 256), :], row_sem.at[g])
        total = total + dot(plb[:, 256 * g : 256 * g + 256], gb[pl.ds(256 * g, 256), :])
    aggregate = (total / counts).astype(BF16)
    na[pl.ds(0, 32), :] = rms_rows(aggregate.astype(F32)).astype(BF16)
    for i in range(1, 4):
        remote(na.at[pl.ds(0, 32), :], na.at[pl.ds(32 * i, 32), :], 4, (dp, lax.rem(x + i, 4))).start()
    for load in loads[7:]:
        load.wait()
    landed(na.at[pl.ds(32, 96), :], recv_sem.at[4])
    hidden = jnp.maximum(s1[...] + dot(na[...], wn[...]), 0.0).astype(BF16)
    to_query, to_head = dot(hidden, wq[...]), dot(hidden, wo[...])
    ps[:, 0:1024] = to_query.astype(BF16)
    ps[:, 1024:1280] = to_head.astype(BF16)
    for i in range(1, 4):
        part = pl.ds(32 * i, 32)
        remote(ps.at[part, :], pr.at[part, :], 5, (dp, lax.rem(x + 4 - i, 4))).start()
    landed(pr.at[pl.ds(32, 96), :], recv_sem.at[5])
    others = (pr[pl.ds(32, 32), :].astype(F32) + pr[pl.ds(64, 32), :].astype(F32)) + pr[pl.ds(96, 32), :].astype(F32)
    terms = jnp.concatenate([to_query[0:32, :], to_head[0:32, :]], axis=1) + others
    queries = terms[:, 0:1024].astype(BF16)
    scores = lax.dot_general(queries, gb[...], (((1,), (1,)), ((), ())), preferred_element_type=F32)
    gates = jnp.where(plb[...].astype(F32) > 0.5, jax.nn.sigmoid(scores * (1.0 / 32.0)), 0.0).astype(BF16)
    context = (dot(gates, gb[...]) / counts).astype(BF16)
    embedding = rms_rows(terms[:, 1024:1280] + dot(context, wc[...])).astype(BF16)
    emb_out[...] = embedding

    slots = dot_first(obt[...], embedding)
    ob[:, 0, :] = slots[0:128, :]
    ob[:, 1, :] = slots[128:256, :]

    def tell(j_first):
        def body(g, _):
            for dp_to, x_to in partners(g, 1)[j_first:]:
                remote(ob.at[dp_to * 4 + x_to], eb.at[me], 6, (dp_to, x_to)).start()
            return 0

        return body

    tell(1)(0, 0)
    lax.fori_loop(1, 8, tell(0), 0)
    own_slots = pltpu.make_async_copy(ob.at[me], eb.at[me], recv_sem.at[6])
    own_slots.start()
    landed(eb, recv_sem.at[6])

    landed(rq.at[pl.ds(0, 127)], send_sem.at[0])
    landed(ns.at[pl.ds(0, 96), :], send_sem.at[2])
    landed(sb.at[pl.ds(16, 2032), :], send_sem.at[3])
    landed(na.at[pl.ds(0, 96), :], send_sem.at[4])
    landed(ps.at[pl.ds(32, 96), :], send_sem.at[5])
    landed(ob.at[pl.ds(0, 127)], send_sem.at[6])


def local(
    features_table, self_features, neighbour_ids, neighbour_counts, node_owner, node_row, list_ids, list_owner,
    list_row, centroids, w_self, w_neigh, w_query, w_out, w_context,
):
    vmem, smem, anyw = (pl.BlockSpec(memory_space=m) for m in (pltpu.VMEM, pltpu.SMEM, pl.ANY))
    i32 = jnp.int32
    scratch = [
        ((2048, 128), i32), ((2048, 128), i32), ((8192, 128), i32), ((8192, 128), i32), ((2048, 1024), BF16),
        ((8192, 256), BF16), ((1024, 512), BF16), ((1024, 512), BF16), ((512, 1024), BF16), ((512, 256), BF16),
        ((1024, 256), BF16),
        ((2048, 256), BF16), ((128, 1, 128), F32), ((128, 1, 128), F32), ((128, 128), BF16), ((32, 128), i32), ((32, 128), i32),
        ((2048, 1024), BF16), ((2048, 1024), BF16), ((32, 2048), BF16), ((32, 256), BF16), ((128, 1024), BF16),
        ((128, 1024), BF16), ((128, 512), F32), ((128, 1280), BF16), ((128, 1280), BF16), ((128, 2, 256), F32),
    ]
    embedding, arrived, centres = pl.pallas_call(
        kernel,
        out_shape=(jax.ShapeDtypeStruct((32, 256), BF16),) + (jax.ShapeDtypeStruct((128, 2, 256), F32),) * 2,
        in_specs=[vmem, vmem, smem, vmem, vmem] + [anyw] * 11,
        out_specs=(vmem, vmem, vmem),
        scratch_shapes=[pltpu.VMEM(s, t) for s, t in scratch]
        + [pltpu.SemaphoreType.DMA((n,)) for n in (11, 8, 8, 8, 8)],
        compiler_params=pltpu.CompilerParams(collective_id=0, has_side_effects=True, vmem_limit_bytes=56 << 20),
    )(
        neighbour_ids, neighbour_counts.reshape(1, 32), list_ids, list_ids.reshape(1, 32), self_features,
        node_owner.reshape(2048, 128), node_row.reshape(2048, 128), list_owner.reshape(8192, 128),
        list_row.reshape(8192, 128), features_table, centroids, w_self, w_neigh, w_query, w_out, w_context,
    )
    return embedding, arrived - centres


def solution(mesh):
    placed = (
        P(("dp", "mp"), None),
        P(("dp", "mp"), None),
        P(("dp", "mp"), None),
        P(("dp", "mp")),
        P(),
        P(),
        P(("dp", "mp")),
        P(),
        P(),
        P(("dp", "mp"), None),
        P(None, "mp"),
        P(None, "mp"),
        P("mp", None),
        P("mp", None),
        P(),
    )
    return jax.shard_map(
        local,
        mesh=mesh,
        in_specs=placed,
        out_specs=(P(("dp", "mp"), None), P(("dp", "mp"), None, None)),
        check_vma=False,
    )
```

time: 107 us -> 96.3 us (0.900)
  Pallas kernels: 99.7 us -> 92.3 us
  local copies, waits for them, and re-layouts: 5.86 us -> 1.32 us
  other arithmetic: 0 us -> 1.87 us
    pallas_call x1, Pallas kernels: 99.7 us -> 92.3 us  [local(): pl.pallas_call(kernel, out_shape=(jax.ShapeDtypeStruct((32, 256), BF16),)...]
    reshape x3 -> x0, local copies, waits for them, and re-layouts: 4.54 us -> none  [the longest x1 1.86 us: local(): return (embedding, residual.reshape(2, 128, 256).transpose(1, 0, 2))]
    sub x0 -> x1, other arithmetic: none -> 1.87 us  [local(): return (embedding, arrived - centres)]
where the time goes in v2:
time: 96.3 us; the launch traced here: 96.1 us
  Pallas kernels  92.3 us (96%)
  other arithmetic  1.87 us (2%)
  local copies, waits for them, and re-layouts  1.32 us (1%)
    pallas_call x1, Pallas kernels, local(): pl.pallas_call(kernel, out_shape=(jax.ShapeDtypeStruct((32, 256), BF16),)...  92.3 us

profile of v2, /device:TPU:1, one launch (start us, length us, event | category | flops | bytes accessed | tf_op | source)
XLA Modules:
  0.0 96.1 jit_solution(408839114337945672)
XLA Ops:
  0.6 92.3 %shard_map.158 = (bf16[32,256]{1,0:T(8,128)(2,1)}, f32[128,2,256]{2,1,0:T(2,128)}, f32[128,2,256]{2,1,0:T(2,128)}) custom-call(s32[32,32]{1,0:T(8,128)} %ids.1, s32[1,32]{1,0:T(1,128)} %bitcast.11, s32[32]{0:T(128)} %lids_s.1, s32[1,32]{1,0:T(1,128)} %bitcast.10, bf16[32,1024]{1,0:T(8,128)(2,1)} %self_f.1, s32[2048,128]{1,0:T(8,128)} %bitcast.8, ...), custom_call_target="tpu_custom_call" | custom-call | tf_op jit(solution)/shard_map/pallas_call | solution.py:315
  92.9 1.9 %sub.3 = f32[128,2,256]{2,1,0:T(2,128)} subtract(f32[128,2,256]{2,1,0:T(2,128)} %get-tuple-element.6, f32[128,2,256]{2,1,0:T(2,128)} %get-tuple-element.7) | non-fusion elementwise | flops 65536 | bytes 786432 | tf_op jit(solution)/shard_map/sub | solution.py:328
  94.8 1.3 %copy.18 = bf16[32,256]{1,0:T(8,128)(2,1)} copy(bf16[32,256]{1,0:T(8,128)(2,1)} %get-tuple-element.10) | data formatting | bytes 32768

commit v3 on v2

--- a/solution.py
+++ b/solution.py
@@ -54,10 +54,10 @@
 
 
 def kernel(
-    ids, cnt, lids_s, lids, self_f, node_owner, node_row, list_owner, list_row, features, centroids,
+    ids_h, cnt_h, lids_h, self_h, node_owner, node_row, list_owner, list_row, features, centroids,
     w_self, w_neigh, w_query, w_out, w_context,
     emb_out, eb, cen,
-    no_v, nr_v, lo_v, lr_v, ft, ct, ws, wn, wq, wo, wc,
+    ids, cnt, lids_s, lids, self_f, no_v, nr_v, lo_v, lr_v, ft, ct, ws, wn, wq, wo, wc,
     btab, rq, rb, held, lo_rows, lr_rows, sb, gb, plb, obt, ns, na, s1, ps, pr, ob, load_sem, send_sem, recv_sem, ask_sem, row_sem,
 ):
     dp, x = lax.axis_index("dp"), lax.axis_index("mp")
@@ -75,6 +75,19 @@
             for j in range(16)
         ]
 
+    barrier = pltpu.get_barrier_semaphore()
+
+    def greet(j_first):
+        def body(g, _):
+            for device in partners(g, 1)[j_first:]:
+                pl.semaphore_signal(barrier, inc=1, device_id=device, device_id_type=MESH)
+            return 0
+
+        return body
+
+    greet(1)(jnp.int32(0), 0)
+    lax.fori_loop(1, 8, greet(0), 0)
+
     loads = [
         pltpu.make_async_copy(src, dst, load_sem.at[i])
         for i, (src, dst) in enumerate(
@@ -82,21 +95,12 @@
              (centroids, ct), (w_neigh, wn), (w_query, wq), (w_out, wo), (w_context, wc)]
         )
     ]
-    for load in loads:
+    small = [
+        pltpu.make_async_copy(src, dst, load_sem.at[11 + i])
+        for i, (src, dst) in enumerate([(ids_h, ids), (cnt_h, cnt), (lids_h.at[0], lids_s), (lids_h, lids), (self_h, self_f)])
+    ]
+    for load in loads[:2] + small + loads[2:]:
         load.start()
-
-    barrier = pltpu.get_barrier_semaphore()
-
-    def greet(j_first):
-        def body(g, _):
-            for device in partners(g, 1)[j_first:]:
-                pl.semaphore_signal(barrier, inc=1, device_id=device, device_id_type=MESH)
-            return 0
-
-        return body
-
-    greet(1)(jnp.int32(0), 0)
-    lax.fori_loop(1, 8, greet(0), 0)
 
     def remote(src, dst, which, device, recv=None):
         return pltpu.make_async_remote_copy(
@@ -107,10 +111,8 @@
     def landed(ref, sem):
         pltpu.make_async_copy(ref, ref, sem).wait()
 
-    ns[pl.ds(0, 32), :] = rms_rows(self_f[...].astype(F32)).astype(BF16)
-
-    loads[0].wait()
-    loads[1].wait()
+    for load in loads[:2] + small:
+        load.wait()
     code = no_v[...] * 2048 + nr_v[...]
     btab[:, 0:128] = (lax.shift_right_logical(code, 9) - 256).astype(F32).astype(BF16)
     btab[:, 128:256] = (jnp.bitwise_and(code, 511) - 256).astype(F32).astype(BF16)
@@ -120,30 +122,37 @@
     lane = iota((256, 128), 1)
     lane_f = lane.astype(F32)
     tri = one_hot(iota((256, 256), 1) < iota((256, 256), 0))
-    carry = jnp.zeros((1, 128), F32)
     slot_row = iota((256, 1), 0)
     node = (lax.rem(slot_row, 32) + 1).astype(F32)
     counts8 = jnp.concatenate([counts] * 8, axis=0)
-    request = jnp.zeros((128, 128), F32)
-    for q in range(4):
-        idc = jnp.concatenate([ids_all[:, 8 * q + j : 8 * q + j + 1] for j in range(8)], axis=0)
-        found = dot(one_hot(iota((256, 2048), 1) == lax.shift_right_logical(idc, 7)), btab[...])
-        sel = lane == jnp.bitwise_and(idc, 127)
-        code = (spread_pick(sel, found[:, 0:128], ones) + 256.0) * 512.0 + (spread_pick(sel, found[:, 128:256], ones) + 256.0)
-        owner = jnp.floor(code * (1.0 / 2048.0))
-        row = code - owner * 2048.0
-        high = jnp.floor(row * (1.0 / 16.0)) * 16.0
-        low = row - high
-        mine = lane_f == owner
-        hot = one_hot(mine)
-        rank = spread_pick(mine, dot(tri, hot) + carry, ones)
-        carry = carry + jnp.sum(jnp.where(mine, 1.0, 0.0), axis=0, keepdims=True)
-        valid = (lax.div(slot_row, 32) + 8 * q).astype(F32) < counts8
-        here = lane_f == rank
-        there = lane_f - 32.0 == rank
-        x_high = jnp.where(here, high, jnp.where(there, jnp.where(valid, node, 0.0), 0.0)).astype(BF16)
-        x_low = jnp.where(here, low, 0.0).astype(BF16)
-        request = request + dot_first(hot, x_high) + dot_first(hot, x_low)
+    four = range(4)
+    idc = [jnp.concatenate([ids_all[:, 8 * q + j : 8 * q + j + 1] for j in range(8)], axis=0) for q in four]
+    found = [dot(one_hot(iota((256, 2048), 1) == lax.shift_right_logical(idc[q], 7)), btab[...]) for q in four]
+    sel = [lane == jnp.bitwise_and(idc[q], 127) for q in four]
+    code = [
+        (spread_pick(sel[q], found[q][:, 0:128], ones) + 256.0) * 512.0
+        + (spread_pick(sel[q], found[q][:, 128:256], ones) + 256.0)
+        for q in four
+    ]
+    owner = [jnp.floor(v * (1.0 / 2048.0)) for v in code]
+    row = [v - o * 2048.0 for v, o in zip(code, owner)]
+    high = [jnp.floor(v * (1.0 / 16.0)) * 16.0 for v in row]
+    low = [v - h for v, h in zip(row, high)]
+    mine = [lane_f == o for o in owner]
+    hot = [one_hot(m) for m in mine]
+    before = [dot(tri, h) for h in hot]
+    sums = [jnp.sum(h.astype(F32), axis=0, keepdims=True) for h in hot]
+    carry = [sum(sums[:q], jnp.zeros((1, 128), F32)) for q in four]
+    rank = [spread_pick(mine[q], before[q] + carry[q], ones) for q in four]
+    valid = [(lax.div(slot_row, 32) + 8 * q).astype(F32) < counts8 for q in four]
+    x_high = [
+        jnp.where(
+            lane_f == rank[q], high[q], jnp.where(lane_f - 32.0 == rank[q], jnp.where(valid[q], node, 0.0), 0.0)
+        ).astype(BF16)
+        for q in four
+    ]
+    x_low = [jnp.where(lane_f == rank[q], low[q], 0.0).astype(BF16) for q in four]
+    request = dot_first(jnp.concatenate(hot * 2, axis=0), jnp.concatenate(x_high + x_low, axis=0))
 
     loads[2].wait()
     loads[3].wait()
@@ -192,6 +201,8 @@
     ask(1)(0, 0)
     lax.fori_loop(1, 8, ask(0), 0)
 
+    ns[pl.ds(0, 32), :] = rms_rows(self_f[...].astype(F32)).astype(BF16)
+
     for i in range(1, 4):
         remote(ns.at[pl.ds(0, 32), :], ns.at[pl.ds(32 * i, 32), :], 2, (dp, lax.rem(x + i, 4))).start()
 
@@ -256,20 +267,27 @@
         load.wait()
     landed(na.at[pl.ds(32, 96), :], recv_sem.at[4])
     hidden = jnp.maximum(s1[...] + dot(na[...], wn[...]), 0.0).astype(BF16)
-    to_query, to_head = dot(hidden, wq[...]), dot(hidden, wo[...])
-    ps[:, 0:1024] = to_query.astype(BF16)
-    ps[:, 1024:1280] = to_head.astype(BF16)
-    for i in range(1, 4):
-        part = pl.ds(32 * i, 32)
-        remote(ps.at[part, :], pr.at[part, :], 5, (dp, lax.rem(x + 4 - i, 4))).start()
-    landed(pr.at[pl.ds(32, 96), :], recv_sem.at[5])
-    others = (pr[pl.ds(32, 32), :].astype(F32) + pr[pl.ds(64, 32), :].astype(F32)) + pr[pl.ds(96, 32), :].astype(F32)
-    terms = jnp.concatenate([to_query[0:32, :], to_head[0:32, :]], axis=1) + others
-    queries = terms[:, 0:1024].astype(BF16)
+    def share(columns, which):
+        for i in range(1, 4):
+            part = (pl.ds(32 * i, 32), columns)
+            remote(ps.at[part], pr.at[part], which, (dp, lax.rem(x + 4 - i, 4))).start()
+
+    def others(columns, which):
+        landed(pr.at[pl.ds(32, 96), columns], recv_sem.at[which])
+        return pr[pl.ds(32, 32), columns].astype(F32) + pr[pl.ds(64, 32), columns].astype(F32) + pr[pl.ds(96, 32), columns].astype(F32)
+
+    for_query, for_head = pl.ds(0, 1024), pl.ds(1024, 256)
+    to_query = dot(hidden, wq[...])
+    ps[:, for_query] = to_query.astype(BF16)
+    share(for_query, 5)
+    to_head = dot(hidden, wo[...])
+    ps[:, for_head] = to_head.astype(BF16)
+    share(for_head, 1)
+    queries = (to_query[0:32, :] + others(for_query, 5)).astype(BF16)
     scores = lax.dot_general(queries, gb[...], (((1,), (1,)), ((), ())), preferred_element_type=F32)
     gates = jnp.where(plb[...].astype(F32) > 0.5, jax.nn.sigmoid(scores * (1.0 / 32.0)), 0.0).astype(BF16)
     context = (dot(gates, gb[...]) / counts).astype(BF16)
-    embedding = rms_rows(terms[:, 1024:1280] + dot(context, wc[...])).astype(BF16)
+    embedding = rms_rows((to_head[0:32, :] + others(for_head, 1)) + dot(context, wc[...])).astype(BF16)
     emb_out[...] = embedding
 
     slots = dot_first(obt[...], embedding)
@@ -294,15 +312,21 @@
     landed(ns.at[pl.ds(0, 96), :], send_sem.at[2])
     landed(sb.at[pl.ds(16, 2032), :], send_sem.at[3])
     landed(na.at[pl.ds(0, 96), :], send_sem.at[4])
-    landed(ps.at[pl.ds(32, 96), :], send_sem.at[5])
+    landed(ps.at[pl.ds(32, 96), for_query], send_sem.at[5])
+    landed(ps.at[pl.ds(32, 96), for_head], send_sem.at[1])
     landed(ob.at[pl.ds(0, 127)], send_sem.at[6])
+
+
+def finish(emb_in, arrived, centres, emb_out, res_out):
+    emb_out[...] = emb_in[...]
+    res_out[...] = arrived[...] - centres[...]
 
 
 def local(
     features_table, self_features, neighbour_ids, neighbour_counts, node_owner, node_row, list_ids, list_owner,
     list_row, centroids, w_self, w_neigh, w_query, w_out, w_context,
 ):
-    vmem, smem, anyw = (pl.BlockSpec(memory_space=m) for m in (pltpu.VMEM, pltpu.SMEM, pl.ANY))
+    vmem, anyw = (pl.BlockSpec(memory_space=m) for m in (pltpu.VMEM, pl.ANY))
     i32 = jnp.int32
     scratch = [
         ((2048, 128), i32), ((2048, 128), i32), ((8192, 128), i32), ((8192, 128), i32), ((2048, 1024), BF16),
@@ -315,17 +339,23 @@
     embedding, arrived, centres = pl.pallas_call(
         kernel,
         out_shape=(jax.ShapeDtypeStruct((32, 256), BF16),) + (jax.ShapeDtypeStruct((128, 2, 256), F32),) * 2,
-        in_specs=[vmem, vmem, smem, vmem, vmem] + [anyw] * 11,
+        in_specs=[anyw] * 15,
         out_specs=(vmem, vmem, vmem),
-        scratch_shapes=[pltpu.VMEM(s, t) for s, t in scratch]
-        + [pltpu.SemaphoreType.DMA((n,)) for n in (11, 8, 8, 8, 8)],
+        scratch_shapes=[pltpu.VMEM((32, 32), i32), pltpu.VMEM((1, 32), i32), pltpu.SMEM((32,), i32), pltpu.VMEM((1, 32), i32), pltpu.VMEM((32, 1024), BF16)]
+        + [pltpu.VMEM(s, t) for s, t in scratch]
+        + [pltpu.SemaphoreType.DMA((n,)) for n in (16, 8, 8, 8, 8)],
         compiler_params=pltpu.CompilerParams(collective_id=0, has_side_effects=True, vmem_limit_bytes=56 << 20),
     )(
-        neighbour_ids, neighbour_counts.reshape(1, 32), list_ids, list_ids.reshape(1, 32), self_features,
+        neighbour_ids, neighbour_counts.reshape(1, 32), list_ids.reshape(1, 32), self_features,
         node_owner.reshape(2048, 128), node_row.reshape(2048, 128), list_owner.reshape(8192, 128),
         list_row.reshape(8192, 128), features_table, centroids, w_self, w_neigh, w_query, w_out, w_context,
     )
-    return embedding, arrived - centres
+    return pl.pallas_call(
+        finish,
+        out_shape=(jax.ShapeDtypeStruct((32, 256), BF16), jax.ShapeDtypeStruct((128, 2, 256), F32)),
+        in_specs=[vmem] * 3,
+        out_specs=(vmem, vmem),
+    )(embedding, arrived, centres)
 
 
 def solution(mesh):

time: 96.3 us -> 93.2 us (0.968)
  other arithmetic: 1.87 us -> 0 us
  local copies, waits for them, and re-layouts: 1.32 us -> 0 us
    sub x1 -> x0, other arithmetic: 1.87 us -> none  [local(): return (embedding, arrived - centres)]
    pallas_call x0 -> x1, Pallas kernels: none -> 1.82 us  [local(): pl.pallas_call(finish, out_shape=(jax.ShapeDtypeStruct((32, 256), BF16),...]
    pallas_call x1, Pallas kernels: 92.3 us -> 90.6 us  [local(): pl.pallas_call(kernel, out_shape=(jax.ShapeDtypeStruct((32, 256), BF16),)...]
    unnamed x1 -> x0, local copies, waits for them, and re-layouts: 1.32 us -> none
where the time goes in v3:
time: 93.2 us; the launch traced here: 93 us
  Pallas kernels  92.4 us (99%)
    pallas_call x1, Pallas kernels, local(): pl.pallas_call(kernel, out_shape=(jax.ShapeDtypeStruct((32, 256), BF16),)...  90.6 us

profile of v3, /device:TPU:1, one launch (start us, length us, event | category | flops | bytes accessed | tf_op | source)
XLA Modules:
  0.0 93.0 jit_solution(13281399994402667630)
XLA Ops:
  0.6 90.6 %shard_map.158 = (bf16[32,256]{1,0:T(8,128)(2,1)}, f32[128,2,256]{2,1,0:T(2,128)}, f32[128,2,256]{2,1,0:T(2,128)}) custom-call(s32[32,32]{1,0:T(8,128)} %ids_h.1, s32[1,32]{1,0:T(1,128)} %bitcast.10, s32[1,32]{1,0:T(1,128)} %bitcast.11, bf16[32,1024]{1,0:T(8,128)(2,1)} %self_h.1, s32[2048,128]{1,0:T(8,128)} %bitcast.8, s32[2048,128]{1,0:T(8,128)} %bitcast.9, ...), custom_call_target="tpu_custom_call" | custom-call | tf_op jit(solution)/shard_map/pallas_call | solution.py:339
  91.2 1.8 %shard_map.159 = (bf16[32,256]{1,0:T(8,128)(2,1)}, f32[128,2,256]{2,1,0:T(2,128)}) custom-call(bf16[32,256]{1,0:T(8,128)(2,1)} %get-tuple-element.5.emb_in, f32[128,2,256]{2,1,0:T(2,128)} %get-tuple-element.6.arrived, f32[128,2,256]{2,1,0:T(2,128)} %get-tuple-element.7.centres), custom_call_target="tpu_custom_call" | custom-call | tf_op jit(solution)/shard_map/pallas_call | solution.py:353

commit v4 on v3

--- a/solution.py
+++ b/solution.py
@@ -58,35 +58,29 @@
     w_self, w_neigh, w_query, w_out, w_context,
     emb_out, eb, cen,
     ids, cnt, lids_s, lids, self_f, no_v, nr_v, lo_v, lr_v, ft, ct, ws, wn, wq, wo, wc,
-    btab, rq, rb, held, lo_rows, lr_rows, sb, gb, plb, obt, ns, na, s1, ps, pr, ob, load_sem, send_sem, recv_sem, ask_sem, row_sem,
+    btab, rq, rb, rl, ll, held, lo_rows, lr_rows, sb, gb, plb, obt, ns, na, s1, ps, pr, ob, cen_v, load_sem, send_sem, recv_sem, ask_sem, row_sem,
 ):
     dp, x = lax.axis_index("dp"), lax.axis_index("mp")
     c, yz = lax.rem(dp, 2), lax.div(dp, 2)
     z, y = lax.rem(yz, 4), lax.div(yz, 4)
     me = dp * 4 + x
 
-    def partners(g, sign):
-        xs = [lax.rem(x + (sign * k) % 4, 4) for k in range(4)]
-        zs = [lax.rem(z + (sign * k) % 4, 4) * 2 for k in range(4)]
-        ys = [lax.rem(y + 16 + sign * (g + k), 4) * 8 for k in range(4)]
-        cs = [lax.rem(c + lax.div(g, 4) + k, 2) for k in range(2)]
+    def turned(at, size, scale):
+        return [lax.rem(at + k, size) * scale for k in range(size)]
+
+    all_x, all_c, all_z, all_y = turned(x, 4, 1), turned(c, 2, 1), turned(z, 4, 2), turned(y, 4, 8)
+
+    def partner(i, sign):
+        g, a, b = i // 16, i % 16 // 4, i % 4
+        y_z = all_y[sign * (g + a + 3 * b) % 4] + all_z[sign * (a + b) % 4]
+        return y_z + all_c[(g // 4 + a + b // 2) % 2], all_x[sign * b % 4]
+
+    def partners(g):
+        ys, cs = turned(y + g, 4, 8), turned(c + lax.div(g, 4), 2, 1)
         return [
-            (ys[(j // 4 + 3 * (j % 4)) % 4] + zs[(j // 4 + j % 4) % 4] + cs[(j // 4 + j % 4 // 2) % 2], xs[j % 4])
+            (ys[(j // 4 + 3 * (j % 4)) % 4] + all_z[(j // 4 + j % 4) % 4] + cs[(j // 4 + j % 4 // 2) % 2], all_x[j % 4])
             for j in range(16)
         ]
-
-    barrier = pltpu.get_barrier_semaphore()
-
-    def greet(j_first):
-        def body(g, _):
-            for device in partners(g, 1)[j_first:]:
-                pl.semaphore_signal(barrier, inc=1, device_id=device, device_id_type=MESH)
-            return 0
-
-        return body
-
-    greet(1)(jnp.int32(0), 0)
-    lax.fori_loop(1, 8, greet(0), 0)
 
     loads = [
         pltpu.make_async_copy(src, dst, load_sem.at[i])
@@ -99,8 +93,17 @@
         pltpu.make_async_copy(src, dst, load_sem.at[11 + i])
         for i, (src, dst) in enumerate([(ids_h, ids), (cnt_h, cnt), (lids_h.at[0], lids_s), (lids_h, lids), (self_h, self_f)])
     ]
-    for load in loads[:2] + small + loads[2:]:
+    for load in small[:2] + loads[:2]:
         load.start()
+
+    barrier = pltpu.get_barrier_semaphore()
+
+    for i in range(1, 128):
+        pl.semaphore_signal(barrier, inc=1, device_id=partner(i, 1), device_id_type=MESH)
+
+    for load in loads[4:5] + small[2:] + loads[2:4] + loads[5:]:
+        load.start()
+
 
     def remote(src, dst, which, device, recv=None):
         return pltpu.make_async_remote_copy(
@@ -111,34 +114,37 @@
     def landed(ref, sem):
         pltpu.make_async_copy(ref, ref, sem).wait()
 
-    for load in loads[:2] + small:
+    def sent_from(i):
+        kx, kc, kz, ky = offset(i)
+        y_z = lax.rem(y + 4 - ky, 4) * 4 + lax.rem(z + 4 - kz, 4)
+        return ((y_z * 2 + lax.rem(c + kc, 2)) * 4 + lax.rem(x + 4 - kx, 4)).astype(F32)
+
+    lane = iota((256, 128), 1)
+    lane_f = lane.astype(F32)
+    partner_lane = sent_from(lane)
+    tri = one_hot(iota((256, 256), 1) < iota((256, 256), 0))
+    ones = jnp.ones((128, 128), BF16)
+    weigh = jnp.where(iota((256, 128), 0) < 128, 512.0, 1.0).astype(BF16)
+    slot_row = iota((256, 1), 0)
+    node = (lax.rem(slot_row, 32) + 1).astype(F32)
+    for load in small[:2] + loads[:2]:
         load.wait()
     code = no_v[...] * 2048 + nr_v[...]
     btab[:, 0:128] = (lax.shift_right_logical(code, 9) - 256).astype(F32).astype(BF16)
     btab[:, 128:256] = (jnp.bitwise_and(code, 511) - 256).astype(F32).astype(BF16)
-    ones = jnp.ones((128, 128), BF16)
     counts = column(cnt[...])
     ids_all = ids[...]
-    lane = iota((256, 128), 1)
-    lane_f = lane.astype(F32)
-    tri = one_hot(iota((256, 256), 1) < iota((256, 256), 0))
-    slot_row = iota((256, 1), 0)
-    node = (lax.rem(slot_row, 32) + 1).astype(F32)
     counts8 = jnp.concatenate([counts] * 8, axis=0)
     four = range(4)
     idc = [jnp.concatenate([ids_all[:, 8 * q + j : 8 * q + j + 1] for j in range(8)], axis=0) for q in four]
     found = [dot(one_hot(iota((256, 2048), 1) == lax.shift_right_logical(idc[q], 7)), btab[...]) for q in four]
-    sel = [lane == jnp.bitwise_and(idc[q], 127) for q in four]
-    code = [
-        (spread_pick(sel[q], found[q][:, 0:128], ones) + 256.0) * 512.0
-        + (spread_pick(sel[q], found[q][:, 128:256], ones) + 256.0)
-        for q in four
-    ]
+    sel = [jnp.bitwise_and(iota((256, 256), 1), 127) == jnp.bitwise_and(idc[q], 127) for q in four]
+    code = [dot(jnp.where(sel[q], found[q], 0.0).astype(BF16), weigh) + float(256 * 512 + 256) for q in four]
     owner = [jnp.floor(v * (1.0 / 2048.0)) for v in code]
     row = [v - o * 2048.0 for v, o in zip(code, owner)]
     high = [jnp.floor(v * (1.0 / 16.0)) * 16.0 for v in row]
     low = [v - h for v, h in zip(row, high)]
-    mine = [lane_f == o for o in owner]
+    mine = [partner_lane == o for o in owner]
     hot = [one_hot(m) for m in mine]
     before = [dot(tri, h) for h in hot]
     sums = [jnp.sum(h.astype(F32), axis=0, keepdims=True) for h in hot]
@@ -154,53 +160,16 @@
     x_low = [jnp.where(lane_f == rank[q], low[q], 0.0).astype(BF16) for q in four]
     request = dot_first(jnp.concatenate(hot * 2, axis=0), jnp.concatenate(x_high + x_low, axis=0))
 
-    loads[2].wait()
-    loads[3].wait()
-
-    def list_lookup(n, _):
-        r = lax.div(lids_s[n], 128)
-        lo_rows[pl.ds(n, 1), :] = lo_v[pl.ds(r, 1), :]
-        lr_rows[pl.ds(n, 1), :] = lr_v[pl.ds(r, 1), :]
-        return 0
-
-    lax.fori_loop(0, 32, list_lookup, 0, unroll=8)
-    lane32 = iota((32, 128), 1)
-    lsel = lane32 == column(jnp.bitwise_and(lids[...], 127)).astype(jnp.int32)
-    dest = pick(lsel, lo_rows[...].astype(F32))
-    lrow = pick(lsel, lr_rows[...].astype(F32)) + 1.0
-    lmine = lane32.astype(F32) == dest
-    lhot = one_hot(lmine)
-    lrank = pick(lmine, dot(one_hot(iota((32, 32), 1) < iota((32, 32), 0)), lhot))
-    lhigh, llow = split16(lrow)
-    lthere = (lane32 - 16).astype(F32) == lrank
-    request = request + dot_first(lhot, jnp.where(lthere, lhigh.astype(F32), 0.0).astype(BF16))
-    request = request + dot_first(lhot, jnp.where(lthere, llow.astype(F32), 0.0).astype(BF16))
-    obt[...] = one_hot(iota((32, 256), 1).astype(F32) == dest + 128.0 * lrank)
-
-    order_row, order_lane = iota((128, 128), 0), iota((128, 128), 1)
-    kx, kc, kz, ky = offset(order_row)
-    from_dp = (lax.rem(y + 4 - ky, 4) * 4 + lax.rem(z + 4 - kz, 4)) * 2 + lax.rem(c + kc, 2)
-    asked = one_hot(order_lane == from_dp * 4 + lax.rem(x + 4 - kx, 4))
-    high, low = split16(request)
-    low = dot(asked, low)
-    held[...] = low.astype(BF16)
-    rq[:, 0, :] = dot(asked, high) + low
+    rq[:, 0, :] = request
+    held[...] = split16(request)[1]
 
     pl.semaphore_wait(barrier, 127)
 
-    def ask(j_first):
-        def body(g, _):
-            for j, device in list(enumerate(partners(g, -1)))[j_first:]:
-                i = 16 * g + j
-                remote(rq.at[i], rb.at[i], 0, device, ask_sem.at[g]).start()
-            return 0
-
-        return body
-
+    for i in range(1, 128):
+        remote(rq.at[i], rb.at[i], 0, partner(i, -1), ask_sem.at[i // 16]).start()
     pltpu.make_async_copy(rq.at[0], rb.at[0], ask_sem.at[0]).start()
-    ask(1)(0, 0)
-    lax.fori_loop(1, 8, ask(0), 0)
-
+
+    small[4].wait()
     ns[pl.ds(0, 32), :] = rms_rows(self_f[...].astype(F32)).astype(BF16)
 
     for i in range(1, 4):
@@ -218,7 +187,7 @@
             index = pick(lane == sub, dot(spread, high) + dot(spread, low)).astype(jnp.int32)
             rows = dot(one_hot(iota((256, 2048), 1) == index), ft[...]).astype(BF16)
             sb[pl.ds(pl.multiple_of(256 * g, 256), 256), :] = rows
-            for j, device in list(enumerate(partners(g, 1)))[j_first:]:
+            for j, device in list(enumerate(partners(g)))[j_first:]:
                 part = pl.ds(pl.multiple_of(256 * g + 16 * j, 16), 16)
                 remote(sb.at[part, :], gb.at[part, :], 3, device, row_sem.at[g]).start()
             return 0
@@ -228,6 +197,33 @@
     serve(1)(0, 0)
     own_rows = pltpu.make_async_copy(sb.at[pl.ds(0, 16), :], gb.at[pl.ds(0, 16), :], row_sem.at[0])
     own_rows.start()
+    for load in small[2:4] + loads[2:4]:
+        load.wait()
+
+    def list_lookup(n, _):
+        r = lax.div(lids_s[n], 128)
+        lo_rows[pl.ds(n, 1), :] = lo_v[pl.ds(r, 1), :]
+        lr_rows[pl.ds(n, 1), :] = lr_v[pl.ds(r, 1), :]
+        return 0
+
+    lax.fori_loop(0, 32, list_lookup, 0, unroll=8)
+    lane32 = iota((32, 128), 1)
+    lsel = lane32 == column(jnp.bitwise_and(lids[...], 127)).astype(jnp.int32)
+    dest = pick(lsel, lo_rows[...].astype(F32))
+    lrow = pick(lsel, lr_rows[...].astype(F32)) + 1.0
+    lmine = sent_from(lane32) == dest
+    lhot = one_hot(lmine)
+    lrank = pick(lmine, dot(one_hot(iota((32, 32), 1) < iota((32, 32), 0)), lhot))
+    lhigh, llow = split16(lrow)
+    lthere = (lane32 - 16).astype(F32) == lrank
+    rl[:, 0, :] = dot_first(lhot, jnp.where(lthere, lhigh.astype(F32), 0.0).astype(BF16)) + dot_first(
+        lhot, jnp.where(lthere, llow.astype(F32), 0.0).astype(BF16)
+    )
+    for i in range(1, 128):
+        remote(rl.at[i], ll.at[i], 7, partner(i, -1)).start()
+    pltpu.make_async_copy(rl.at[0], ll.at[0], recv_sem.at[7]).start()
+    obt[...] = one_hot(iota((32, 256), 1).astype(F32) == dest + 128.0 * lrank)
+
     lax.fori_loop(1, 8, serve(0), 0)
 
     for g in range(8):
@@ -240,10 +236,12 @@
     loads[5].wait()
     s1[...] = dot(ns[...], ws[...])
     loads[6].wait()
+    order_row, order_lane = iota((128, 128), 0), iota((128, 128), 1)
     kx, kc, kz, ky = offset(order_lane)
     to_dp = (lax.rem(y + ky, 4) * 4 + lax.rem(z + kz, 4)) * 2 + lax.rem(c + kc, 2)
     by_source = one_hot(order_row == to_dp * 4 + lax.rem(x + kx, 4))
-    high, low = split16(rb[:, 0, :])
+    landed(ll, recv_sem.at[7])
+    high, low = split16(ll[:, 0, :])
     lists = dot(by_source, high) + dot(by_source, low)
     wanted = jnp.concatenate([lists[:, 16:17], lists[:, 17:18]], axis=0).astype(jnp.int32) - 1
 
@@ -252,8 +250,10 @@
         return total + dot(hot, ct[pl.ds(pl.multiple_of(1024 * k, 1024), 1024), :])
 
     centres = lax.fori_loop(0, 8, centre, jnp.zeros((256, 256), F32))
-    cen[:, 0, :] = centres[0:128, :]
-    cen[:, 1, :] = centres[128:256, :]
+    cen_v[:, 0, :] = centres[0:128, :]
+    cen_v[:, 1, :] = centres[128:256, :]
+    keep = pltpu.make_async_copy(cen_v, cen, recv_sem.at[0])
+    keep.start()
 
     total = jnp.zeros((32, 1024), F32)
     for g in range(8):
@@ -294,20 +294,14 @@
     ob[:, 0, :] = slots[0:128, :]
     ob[:, 1, :] = slots[128:256, :]
 
-    def tell(j_first):
-        def body(g, _):
-            for dp_to, x_to in partners(g, 1)[j_first:]:
-                remote(ob.at[dp_to * 4 + x_to], eb.at[me], 6, (dp_to, x_to)).start()
-            return 0
-
-        return body
-
-    tell(1)(0, 0)
-    lax.fori_loop(1, 8, tell(0), 0)
+    for i in range(1, 128):
+        dp_to, x_to = partner(i, 1)
+        remote(ob.at[dp_to * 4 + x_to], eb.at[me], 6, (dp_to, x_to)).start()
     own_slots = pltpu.make_async_copy(ob.at[me], eb.at[me], recv_sem.at[6])
     own_slots.start()
     landed(eb, recv_sem.at[6])
 
+    keep.wait()
     landed(rq.at[pl.ds(0, 127)], send_sem.at[0])
     landed(ns.at[pl.ds(0, 96), :], send_sem.at[2])
     landed(sb.at[pl.ds(16, 2032), :], send_sem.at[3])
@@ -315,6 +309,7 @@
     landed(ps.at[pl.ds(32, 96), for_query], send_sem.at[5])
     landed(ps.at[pl.ds(32, 96), for_head], send_sem.at[1])
     landed(ob.at[pl.ds(0, 127)], send_sem.at[6])
+    landed(rl.at[pl.ds(0, 127)], send_sem.at[7])
 
 
 def finish(emb_in, arrived, centres, emb_out, res_out):
@@ -332,15 +327,15 @@
         ((2048, 128), i32), ((2048, 128), i32), ((8192, 128), i32), ((8192, 128), i32), ((2048, 1024), BF16),
         ((8192, 256), BF16), ((1024, 512), BF16), ((1024, 512), BF16), ((512, 1024), BF16), ((512, 256), BF16),
         ((1024, 256), BF16),
-        ((2048, 256), BF16), ((128, 1, 128), F32), ((128, 1, 128), F32), ((128, 128), BF16), ((32, 128), i32), ((32, 128), i32),
+        ((2048, 256), BF16), ((128, 1, 128), F32), ((128, 1, 128), F32), ((128, 1, 128), F32), ((128, 1, 128), F32), ((128, 128), BF16), ((32, 128), i32), ((32, 128), i32),
         ((2048, 1024), BF16), ((2048, 1024), BF16), ((32, 2048), BF16), ((32, 256), BF16), ((128, 1024), BF16),
-        ((128, 1024), BF16), ((128, 512), F32), ((128, 1280), BF16), ((128, 1280), BF16), ((128, 2, 256), F32),
+        ((128, 1024), BF16), ((128, 512), F32), ((128, 1280), BF16), ((128, 1280), BF16), ((128, 2, 256), F32), ((128, 2, 256), F32),
     ]
     embedding, arrived, centres = pl.pallas_call(
         kernel,
         out_shape=(jax.ShapeDtypeStruct((32, 256), BF16),) + (jax.ShapeDtypeStruct((128, 2, 256), F32),) * 2,
         in_specs=[anyw] * 15,
-        out_specs=(vmem, vmem, vmem),
+        out_specs=(vmem, vmem, anyw),
         scratch_shapes=[pltpu.VMEM((32, 32), i32), pltpu.VMEM((1, 32), i32), pltpu.SMEM((32,), i32), pltpu.VMEM((1, 32), i32), pltpu.VMEM((32, 1024), BF16)]
         + [pltpu.VMEM(s, t) for s, t in scratch]
         + [pltpu.SemaphoreType.DMA((n,)) for n in (16, 8, 8, 8, 8)],

time: 93.2 us -> 91.8 us (0.985)
  Pallas kernels: 92.4 us -> 91 us
    pallas_call x1, Pallas kernels: 90.6 us -> 89.2 us  [local(): pl.pallas_call(kernel, out_shape=(jax.ShapeDtypeStruct((32, 256), BF16),)...]
where the time goes in v4:
time: 91.8 us; the launch traced here: 91.6 us
  Pallas kernels  91 us (99%)
    pallas_call x1, Pallas kernels, local(): pl.pallas_call(kernel, out_shape=(jax.ShapeDtypeStruct((32, 256), BF16),)...  89.2 us

profile of v4, /device:TPU:1, one launch (start us, length us, event | category | flops | bytes accessed | tf_op | source)
XLA Modules:
  0.0 91.6 jit_solution(15244058400439681621)
XLA Ops:
  0.6 89.2 %shard_map.158 = (bf16[32,256]{1,0:T(8,128)(2,1)}, f32[128,2,256]{2,1,0:T(2,128)}, f32[128,2,256]{2,1,0:T(2,128)}) custom-call(s32[32,32]{1,0:T(8,128)} %ids_h.1, s32[1,32]{1,0:T(1,128)} %bitcast.10, s32[1,32]{1,0:T(1,128)} %bitcast.11, bf16[32,1024]{1,0:T(8,128)(2,1)} %self_h.1, s32[2048,128]{1,0:T(8,128)} %bitcast.8, s32[2048,128]{1,0:T(8,128)} %bitcast.9, ...), custom_call_target="tpu_custom_call" | custom-call | tf_op jit(solution)/shard_map/pallas_call | solution.py:334
  89.8 1.8 %shard_map.159 = (bf16[32,256]{1,0:T(8,128)(2,1)}, f32[128,2,256]{2,1,0:T(2,128)}) custom-call(bf16[32,256]{1,0:T(8,128)(2,1)} %get-tuple-element.5.emb_in, f32[128,2,256]{2,1,0:T(2,128)} %get-tuple-element.6.arrived, f32[128,2,256]{2,1,0:T(2,128)} %get-tuple-element.7.centres), custom_call_target="tpu_custom_call" | custom-call | tf_op jit(solution)/shard_map/pallas_call | solution.py:348

commit v5 on v4

--- a/solution.py
+++ b/solution.py
@@ -101,7 +101,7 @@
     for i in range(1, 128):
         pl.semaphore_signal(barrier, inc=1, device_id=partner(i, 1), device_id_type=MESH)
 
-    for load in loads[4:5] + small[2:] + loads[2:4] + loads[5:]:
+    for load in loads[4:5] + small[2:]:
         load.start()
 
 
@@ -168,6 +168,8 @@
     for i in range(1, 128):
         remote(rq.at[i], rb.at[i], 0, partner(i, -1), ask_sem.at[i // 16]).start()
     pltpu.make_async_copy(rq.at[0], rb.at[0], ask_sem.at[0]).start()
+    for load in loads[2:4]:
+        load.start()
 
     small[4].wait()
     ns[pl.ds(0, 32), :] = rms_rows(self_f[...].astype(F32)).astype(BF16)
@@ -224,6 +226,8 @@
     pltpu.make_async_copy(rl.at[0], ll.at[0], recv_sem.at[7]).start()
     obt[...] = one_hot(iota((32, 256), 1).astype(F32) == dest + 128.0 * lrank)
 
+    for load in loads[5:]:
+        load.start()
     lax.fori_loop(1, 8, serve(0), 0)
 
     for g in range(8):

time: 91.8 us -> 91.8 us (level)
  no operation moved by 1% of the time
where the time goes in v5:
time: 91.8 us; the launch traced here: 91.7 us
  Pallas kernels  91 us (99%)
    pallas_call x1, Pallas kernels, local(): pl.pallas_call(kernel, out_shape=(jax.ShapeDtypeStruct((32, 256), BF16),)...  89.2 us

profile of v5, /device:TPU:1, one launch (start us, length us, event | category | flops | bytes accessed | tf_op | source)
XLA Modules:
  0.0 91.7 jit_solution(659192631624064225)
XLA Ops:
  0.6 89.2 %shard_map.158 = (bf16[32,256]{1,0:T(8,128)(2,1)}, f32[128,2,256]{2,1,0:T(2,128)}, f32[128,2,256]{2,1,0:T(2,128)}) custom-call(s32[32,32]{1,0:T(8,128)} %ids_h.1, s32[1,32]{1,0:T(1,128)} %bitcast.10, s32[1,32]{1,0:T(1,128)} %bitcast.11, bf16[32,1024]{1,0:T(8,128)(2,1)} %self_h.1, s32[2048,128]{1,0:T(8,128)} %bitcast.8, s32[2048,128]{1,0:T(8,128)} %bitcast.9, ...), custom_call_target="tpu_custom_call" | custom-call | tf_op jit(solution)/shard_map/pallas_call | solution.py:338
  89.8 1.8 %shard_map.159 = (bf16[32,256]{1,0:T(8,128)(2,1)}, f32[128,2,256]{2,1,0:T(2,128)}) custom-call(bf16[32,256]{1,0:T(8,128)(2,1)} %get-tuple-element.5.emb_in, f32[128,2,256]{2,1,0:T(2,128)} %get-tuple-element.6.arrived, f32[128,2,256]{2,1,0:T(2,128)} %get-tuple-element.7.centres), custom_call_target="tpu_custom_call" | custom-call | tf_op jit(solution)/shard_map/pallas_call | solution.py:352
